TPU v7x, 32 devices: a whole 2x2x4 slice. The times are simulated.
32 devices in a mesh: pair: 2 (over core), grp: 4 (over z), sp: 4 (over y, x).
Axes of the slice: x: 2, y: 2, z: 4, core: 2. Of those that a mesh axis runs over, the one named last changes fastest.
Arguments:
- tokens: bfloat16 [2, 1024, 64, 128], P('pair', ('grp', 'sp')), may hold values from -6 to 6
- owner_ids: int32 [2, 1024, 2], P('pair', ('grp', 'sp')), may hold values from 0 to 15, all different within a row; in each aligned block of 64 rows (0 to 63, 64 to 127, ..., all dimensions but the last counted through in order) at most 16 rows name the same one
- local_ids: int32 [2, 1024, 2], P('pair', ('grp', 'sp')), may hold values from 0 to 63
- weight_qkv: bfloat16 [128, 384], replicated, may hold values from -64 to 64
- weight_out: bfloat16 [128, 128], replicated, may hold values from -0.5 to 0.5
- weight_up: bfloat16 [128, 512], replicated, may hold values from -0.5 to 0.5
- weight_down: bfloat16 [512, 128], replicated, may hold values from -0.25 to 0.25
- cotangent: bfloat16 [2, 1024, 64, 128], P('pair', ('grp', 'sp')), may hold values from -6 to 6
Outputs:
- block_out: bfloat16 [2, 1024, 64, 128], P('pair', ('grp', 'sp'))
- grad_tokens: bfloat16 [2, 1024, 64, 128], P('pair', ('grp', 'sp'))
- grad_qkv: float32 [128, 384], replicated
- grad_out: float32 [128, 128], replicated
- grad_up: float32 [128, 512], replicated
- grad_down: float32 [512, 128], replicated
Inputs may be any that keep to these rules, and one draw needn't show every extreme that they name: `owner_ids`: each window names 2 different devices; among the 64 windows of one device no device is named more than 16 times, and some device exactly 16 times.
All inputs are finite; a program needn't handle non-finite values.
Results may differ from a plain program's by a relative error of at most 0.006.
The roundings to bfloat16 on the way count: a program that leaves them out, or rounds other values in their place, can miss the bound.
Values may be sent and summed in bfloat16 or wider, within the bound.
A program may use at most 128 MiB of HBM per device.

v0:
```python
import math

import jax
import jax.numpy as jnp
from jax import lax
from jax.sharding import PartitionSpec as P

HEADS = 4


eps_norm = 1e-05
gelu_scale = 0.7978845608028654
gelu_cubic = 0.044715


def swapped(value, axis, stride):
    mask = 2**stride
    pairs = [(source, source ^ mask) for source in range(lax.axis_size(axis))]
    return lax.ppermute(value, axis, pairs)


def norm_rows(values):
    centred = values - jnp.mean(values, axis=-1, keepdims=True)
    factor = lax.rsqrt(jnp.mean(centred * centred, axis=-1, keepdims=True) + eps_norm)
    return (centred * factor, factor)


def norm_back(upstream, normed, factor):
    return factor * (
        upstream
        - jnp.mean(upstream, axis=-1, keepdims=True)
        - normed * jnp.mean(upstream * normed, axis=-1, keepdims=True)
    )


def gelu_pair(upper):
    tangent = jnp.tanh(gelu_scale * (upper + gelu_cubic * upper * upper * upper))
    value = 0.5 * upper * (1.0 + tangent)
    slope = 0.5 * (1.0 + tangent) + 0.5 * upper * (1.0 - tangent * tangent) * gelu_scale * (
        1.0 + 3.0 * gelu_cubic * upper * upper
    )
    return (value, slope)


def matmul(former, latter):
    return jnp.dot(former, latter, preferred_element_type=jnp.float32)


def against(former, latter):
    return lax.dot_general(
        former, latter, (((1,), (1,)), ((), ())), preferred_element_type=jnp.float32
    )


def outer_sum(former, latter):
    return lax.dot_general(
        former, latter, (((0,), (0,)), ((), ())), preferred_element_type=jnp.float32
    )


def softmax_rows(scores):
    peak = jnp.max(scores, axis=-1, keepdims=True)
    powers = jnp.exp(scores - peak)
    return powers / jnp.sum(powers, axis=-1, keepdims=True)


def split_heads(values, heads):
    return values.reshape(values.shape[0], values.shape[1], heads, values.shape[2] // heads)


def attend(query, kv_cat, heads):
    width = query.shape[-1]
    factor = 1.0 / math.sqrt(width // heads)
    head_query = split_heads(query, heads)
    head_keys = split_heads(kv_cat[..., :width], heads)
    head_values = split_heads(kv_cat[..., width:], heads)
    weights = softmax_rows(
        jnp.einsum("nqhd,nkhd->nhqk", head_query, head_keys, preferred_element_type=jnp.float32)
        * factor
    )
    mixed = jnp.einsum(
        "nhqk,nkhd->nqhd",
        weights.astype(jnp.bfloat16),
        head_values,
        preferred_element_type=jnp.float32,
    )
    return mixed.reshape(query.shape).astype(jnp.bfloat16)


def attend_back(query, kv_cat, grad_mixed, heads, window_len):
    items, span = (kv_cat.shape[0], kv_cat.shape[1])
    width = query.shape[-1]
    factor = 1.0 / math.sqrt(width // heads)
    head_query = split_heads(query, heads)
    head_keys = split_heads(kv_cat[..., :width], heads)
    head_values = split_heads(kv_cat[..., width:], heads)
    head_grad = split_heads(grad_mixed, heads)
    weights = softmax_rows(
        jnp.einsum("nqhd,nkhd->nhqk", head_query, head_keys, preferred_element_type=jnp.float32)
        * factor
    )
    weights_low = weights.astype(jnp.bfloat16)
    grad_weights = jnp.einsum(
        "nqhd,nkhd->nhqk", head_grad, head_values, preferred_element_type=jnp.float32
    )
    centred = grad_weights - jnp.sum(grad_weights * weights, axis=-1, keepdims=True)
    grad_scores = (weights * centred * factor).astype(jnp.bfloat16)
    grad_query = jnp.einsum(
        "nhqk,nkhd->nqhd", grad_scores, head_keys, preferred_element_type=jnp.float32
    ).reshape(query.shape)
    grad_keys = jnp.einsum(
        "nhqk,nqhd->nkhd", grad_scores, head_query, preferred_element_type=jnp.float32
    ).reshape(items, span, width)
    grad_values = jnp.einsum(
        "nhqk,nqhd->nkhd", weights_low, head_grad, preferred_element_type=jnp.float32
    ).reshape(items, span, width)
    grad_kv = jnp.concatenate([grad_keys, grad_values], axis=-1).reshape(
        items, span // window_len, window_len, 2 * width
    )
    return (grad_query, grad_kv[:, 0], grad_kv[:, 1:].astype(jnp.bfloat16))


def tail_forward(rows, mixed, weight_out, weight_up, weight_down):
    resid = lax.optimization_barrier(
        (rows.astype(jnp.float32) + matmul(mixed, weight_out)).astype(jnp.bfloat16)
    )
    normed2, factor2 = norm_rows(resid.astype(jnp.float32))
    normed_low = normed2.astype(jnp.bfloat16)
    value, slope = gelu_pair(matmul(normed_low, weight_up))
    act = value.astype(jnp.bfloat16)
    out_rows = (resid.astype(jnp.float32) + matmul(act, weight_down)).astype(jnp.bfloat16)
    return (out_rows, (normed2, factor2, normed_low, slope, act))


def tail_backward(cot_rows, mixed, saved, weight_out, weight_up, weight_down):
    normed2, factor2, normed_low, slope, act = saved
    grad_upper = (against(cot_rows, weight_down) * slope).astype(jnp.bfloat16)
    grad_resid = cot_rows.astype(jnp.float32) + norm_back(
        against(grad_upper, weight_up), normed2, factor2
    )
    grad_resid_low = grad_resid.astype(jnp.bfloat16)
    grad_mixed = against(grad_resid_low, weight_out).astype(jnp.bfloat16)
    grads = (
        outer_sum(mixed, grad_resid_low),
        outer_sum(normed_low, grad_upper),
        outer_sum(act, cot_rows),
    )
    return (grad_resid, grad_mixed, grads)


def deliver(parcel):
    return lax.all_to_all(parcel, ("grp", "sp"), split_axis=0, concat_axis=0, tiled=True)


def body(tokens, owner_ids, local_ids, weight_qkv, weight_out, weight_up, weight_down, cotangent):
    holders = lax.axis_size("grp") * lax.axis_size("sp")
    width = tokens.shape[-1]
    windows = tokens.shape[1]
    window_len = tokens.shape[2]
    fanout = owner_ids.shape[-1]
    slots = max(2, 2 * windows * fanout // holders)
    keys_len = (fanout + 1) * window_len
    rows_total = windows * window_len
    group_size = 8
    row_blocks = windows // group_size
    token_rows = tokens[0].reshape(rows_total, width)
    cot_rows = cotangent[0].reshape(rows_total, width)
    normed1, factor1 = norm_rows(token_rows.astype(jnp.float32))
    normed1_low = normed1.astype(jnp.bfloat16)
    qkv = (
        matmul(normed1_low, weight_qkv).astype(jnp.bfloat16).reshape(windows, window_len, 3 * width)
    )
    query = qkv[..., :width]
    own_kv = qkv[..., width:]
    owners = owner_ids[0].reshape(-1)
    local_rows = local_ids[0].reshape(-1)
    onehot = (owners[:, None] == jnp.arange(holders, dtype=jnp.int32)[None, :]).astype(jnp.int32)
    ranks = jnp.sum((jnp.cumsum(onehot, axis=0) - 1) * onehot, axis=1)
    position = owners * slots + ranks
    requests = (
        jnp.full((holders * slots,), windows, jnp.int32)
        .at[position]
        .set(local_rows)
        .reshape(holders, slots)
    )
    outgoing = swapped(requests, "pair", 0)
    wanted = lax.all_to_all(outgoing, ("grp", "sp"), split_axis=0, concat_axis=0, tiled=True)
    wanted_flat = wanted.reshape(-1)
    picked = jnp.take(own_kv, wanted_flat, axis=0, mode="clip").reshape(
        holders, slots, window_len, 2 * width
    )
    answered = deliver(picked)
    answered = swapped(answered, "pair", 0)
    far_rows = answered.reshape(holders * slots, window_len, 2 * width)[position]
    far_rows = far_rows.reshape(windows, fanout, window_len, 2 * width)
    kv_cat = jnp.concatenate([own_kv[:, None], far_rows], axis=1).reshape(
        windows, keys_len, 2 * width
    )
    query_groups = query.reshape(row_blocks, group_size, window_len, width)
    kv_groups = kv_cat.reshape(row_blocks, group_size, keys_len, 2 * width)

    def forward_group(inputs):
        return attend(inputs[0], inputs[1], HEADS)

    mixed = lax.map(forward_group, (query_groups, kv_groups)).reshape(rows_total, width)
    out_rows, saved = tail_forward(token_rows, mixed, weight_out, weight_up, weight_down)
    grad_resid, grad_mixed, grads = tail_backward(
        cot_rows, mixed, saved, weight_out, weight_up, weight_down
    )
    grad_groups = grad_mixed.reshape(row_blocks, group_size, window_len, width)

    def backward_group(inputs):
        return attend_back(inputs[0], inputs[1], inputs[2], HEADS, window_len)

    grad_query, self_grad, far_grad = lax.map(
        backward_group, (query_groups, kv_groups, grad_groups)
    )
    self_grad = self_grad.reshape(windows, window_len, 2 * width)
    far_grad = far_grad.reshape(windows * fanout, window_len, 2 * width)
    outbound = (
        jnp.zeros((holders * slots, window_len, 2 * width), jnp.bfloat16).at[position].set(far_grad)
    )
    outbound = outbound.reshape(holders, slots, window_len, 2 * width)
    returned = deliver(swapped(outbound, "pair", 0))
    returned_up = returned.reshape(holders * slots, window_len, 2 * width).astype(jnp.float32)
    kv_grad = self_grad.at[wanted_flat].add(returned_up, mode="drop")
    grad_rows_qkv = jnp.concatenate(
        [grad_query.reshape(rows_total, width), kv_grad.reshape(rows_total, 2 * width)], axis=1
    ).astype(jnp.bfloat16)
    qkv_part = outer_sum(normed1_low, grad_rows_qkv)
    grad_rows = (
        grad_resid + norm_back(against(grad_rows_qkv, weight_qkv), normed1, factor1)
    ).astype(jnp.bfloat16)
    totals = lax.psum((qkv_part, grads[0], grads[1], grads[2]), ("pair", "grp", "sp"))
    inv_count = 1.0 / math.sqrt(2 * windows * holders * window_len)
    block_out = out_rows.reshape(1, windows, window_len, width)
    grad_tokens = grad_rows.reshape(1, windows, window_len, width)
    return (
        block_out,
        grad_tokens,
        totals[0] * inv_count,
        totals[1] * inv_count,
        totals[2] * inv_count,
        totals[3] * inv_count,
    )


def solution(mesh):
    in_specs = (
        P("pair", ("grp", "sp"), None, None),
        P("pair", ("grp", "sp"), None),
        P("pair", ("grp", "sp"), None),
        P(),
        P(),
        P(),
        P(),
        P("pair", ("grp", "sp"), None, None),
    )
    out_specs = (
        P("pair", ("grp", "sp"), None, None),
        P("pair", ("grp", "sp"), None, None),
        P(),
        P(),
        P(),
        P(),
    )
    return jax.shard_map(body, mesh=mesh, in_specs=in_specs, out_specs=out_specs, check_vma=False)
```

profile of v0, /device:TPU:0, one launch (start us, length us, event | category | flops | bytes accessed | tf_op | source)
XLA Modules:
  0.0 1182.2 jit_solution(13464180359263124510)
XLA Ops:
  19.3 7.9 all-to-all-start
  35.7 8.4 gather_fusion
  44.2 188.3 %all_to_all.19 = bf16[16,16,64,256]{3,2,1,0:T(8,128)(2,1)} all-to-all(bf16[16,16,64,256]{3,2,1,0:T(8,128)(2,1)} %bitcast.162), channel_id=1, replica_groups=mesh['pair'=2,'grp'=4,'sp'=4] {'grp','sp'}, dimensions={0} | all-to-all | bytes 16777216 | tf_op jit(solution)/shard_map/all_to_all | solution.py:152
  235.6 10.3 collective-permute-done.1
  245.9 6.3 gather_fusion.1
  257.7 10.8 copy.37
  268.5 37.6 %while.24 = (s32[]{:T(128)}, bf16[8,8,64,128]{3,2,1,0:T(8,128)(2,1)}, bf16[8,8,192,256]{2,3,1,0:T(8,128)(2,1)}, bf16[8,8,64,128]{2,3,1,0:T(8,128)(2,1)}, s32[]{:T(128)}) while((s32[]{:T(128)}, bf16[8,8,64,128]{3,2,1,0:T(8,128)(2,1)}, bf16[8,8,192,256]{2,3,1,0:T(8,128)(2,1)}, bf16[8,8,64,128]{2,3,1,0:T(8,128)(2,1)}, s32[]{:T(128)}) %tuple.59), condition=%wide.region_8.9_spmd, body=%wide.region_5.8_spmd.sunk | while | flops 52363456 | bytes 8143429 | solution.py:205
  315.3 5.7 fusion.44
  328.8 404.6 %while.25 = (s32[]{:T(128)}, bf16[8,8,64,128]{3,2,1,0:T(8,128)(2,1)}, f32[8,8,64,256]{3,2,1,0:T(8,128)}, bf16[8,8,2,64,256]{4,3,2,1,0:T(8,128)(2,1)}, bf16[8,8,1...) while((s32[]{:T(128)}, ...), condition=%wide.region_17.18_spmd, body=%wide.region_13.17_spmd.sunk | while | flops 134484544 | bytes 46171884 | solution.py:215
  342.8 14.5 %fusion.151 = f32[8,192,4,32]{1,3,2,0:T(8,128)} fusion(bf16[8,64,4,32]{1,3,2,0:T(8,128)(2,1)} %bitcast.165, f32[8,4,64,192]{3,2,1,0:T(8,128)S(1)} %fusion.148, f32[8,4,64,192]{3,2,1,0:T(8,128)} %copy-done.3, f32[8,4,64]{2,1,0:T(4,128)S(1)} %get-tuple-element.229), kind=kOutput, calls=%fused_computation.29.clone.1 | convolution fusion | flops 27920576 | bytes 4071424 | tf_op jit(solution)/shard_map/while/body/eval_jaxpr/nhqk,nqhd->nkhd/dot_general | solution.py:111
  364.0 14.7 %fusion.150 = bf16[8,4,32,64]{3,2,1,0:T(8,128)(2,1)S(1)} fusion(bf16[8,192,4,32]{1,3,2,0:T(8,128)(2,1)S(1)} %bitcast.159, f32[8,4,64,192]{3,2,1,0:T(8,128)} %copy-done.4, f32[8,4,64,192]{3,2,1,0:T(8,128)} %copy-done.3, f32[8,4,64]{2,1,0:T(4,128)S(1)} %get-tuple-element.229), kind=kOutput, calls=%fused_computation.26.clone.1 | convolution fusion | flops 27920576 | bytes 3678208 | tf_op jit(solution)/shard_map/while/body/eval_jaxpr/nhqk,nkhd->nqhd/dot_general | solution.py:108
  393.3 14.5 %fusion.151 = f32[8,192,4,32]{1,3,2,0:T(8,128)} fusion(bf16[8,64,4,32]{1,3,2,0:T(8,128)(2,1)} %bitcast.165, f32[8,4,64,192]{3,2,1,0:T(8,128)S(1)} %fusion.148, f32[8,4,64,192]{3,2,1,0:T(8,128)} %copy-done.3, f32[8,4,64]{2,1,0:T(4,128)S(1)} %get-tuple-element.229), kind=kOutput, calls=%fused_computation.29.clone.1 | convolution fusion | flops 27920576 | bytes 4071424 | tf_op jit(solution)/shard_map/while/body/eval_jaxpr/nhqk,nqhd->nkhd/dot_general | solution.py:111
  414.6 14.7 %fusion.150 = bf16[8,4,32,64]{3,2,1,0:T(8,128)(2,1)S(1)} fusion(bf16[8,192,4,32]{1,3,2,0:T(8,128)(2,1)S(1)} %bitcast.159, f32[8,4,64,192]{3,2,1,0:T(8,128)} %copy-done.4, f32[8,4,64,192]{3,2,1,0:T(8,128)} %copy-done.3, f32[8,4,64]{2,1,0:T(4,128)S(1)} %get-tuple-element.229), kind=kOutput, calls=%fused_computation.26.clone.1 | convolution fusion | flops 27920576 | bytes 3678208 | tf_op jit(solution)/shard_map/while/body/eval_jaxpr/nhqk,nkhd->nqhd/dot_general | solution.py:108
  443.9 14.5 %fusion.151 = f32[8,192,4,32]{1,3,2,0:T(8,128)} fusion(bf16[8,64,4,32]{1,3,2,0:T(8,128)(2,1)} %bitcast.165, f32[8,4,64,192]{3,2,1,0:T(8,128)S(1)} %fusion.148, f32[8,4,64,192]{3,2,1,0:T(8,128)} %copy-done.3, f32[8,4,64]{2,1,0:T(4,128)S(1)} %get-tuple-element.229), kind=kOutput, calls=%fused_computation.29.clone.1 | convolution fusion | flops 27920576 | bytes 4071424 | tf_op jit(solution)/shard_map/while/body/eval_jaxpr/nhqk,nqhd->nkhd/dot_general | solution.py:111
  465.1 14.7 %fusion.150 = bf16[8,4,32,64]{3,2,1,0:T(8,128)(2,1)S(1)} fusion(bf16[8,192,4,32]{1,3,2,0:T(8,128)(2,1)S(1)} %bitcast.159, f32[8,4,64,192]{3,2,1,0:T(8,128)} %copy-done.4, f32[8,4,64,192]{3,2,1,0:T(8,128)} %copy-done.3, f32[8,4,64]{2,1,0:T(4,128)S(1)} %get-tuple-element.229), kind=kOutput, calls=%fused_computation.26.clone.1 | convolution fusion | flops 27920576 | bytes 3678208 | tf_op jit(solution)/shard_map/while/body/eval_jaxpr/nhqk,nkhd->nqhd/dot_general | solution.py:108
  494.4 14.5 %fusion.151 = f32[8,192,4,32]{1,3,2,0:T(8,128)} fusion(bf16[8,64,4,32]{1,3,2,0:T(8,128)(2,1)} %bitcast.165, f32[8,4,64,192]{3,2,1,0:T(8,128)S(1)} %fusion.148, f32[8,4,64,192]{3,2,1,0:T(8,128)} %copy-done.3, f32[8,4,64]{2,1,0:T(4,128)S(1)} %get-tuple-element.229), kind=kOutput, calls=%fused_computation.29.clone.1 | convolution fusion | flops 27920576 | bytes 4071424 | tf_op jit(solution)/shard_map/while/body/eval_jaxpr/nhqk,nqhd->nkhd/dot_general | solution.py:111
  515.7 14.7 %fusion.150 = bf16[8,4,32,64]{3,2,1,0:T(8,128)(2,1)S(1)} fusion(bf16[8,192,4,32]{1,3,2,0:T(8,128)(2,1)S(1)} %bitcast.159, f32[8,4,64,192]{3,2,1,0:T(8,128)} %copy-done.4, f32[8,4,64,192]{3,2,1,0:T(8,128)} %copy-done.3, f32[8,4,64]{2,1,0:T(4,128)S(1)} %get-tuple-element.229), kind=kOutput, calls=%fused_computation.26.clone.1 | convolution fusion | flops 27920576 | bytes 3678208 | tf_op jit(solution)/shard_map/while/body/eval_jaxpr/nhqk,nkhd->nqhd/dot_general | solution.py:108
  545.0 14.5 %fusion.151 = f32[8,192,4,32]{1,3,2,0:T(8,128)} fusion(bf16[8,64,4,32]{1,3,2,0:T(8,128)(2,1)} %bitcast.165, f32[8,4,64,192]{3,2,1,0:T(8,128)S(1)} %fusion.148, f32[8,4,64,192]{3,2,1,0:T(8,128)} %copy-done.3, f32[8,4,64]{2,1,0:T(4,128)S(1)} %get-tuple-element.229), kind=kOutput, calls=%fused_computation.29.clone.1 | convolution fusion | flops 27920576 | bytes 4071424 | tf_op jit(solution)/shard_map/while/body/eval_jaxpr/nhqk,nqhd->nkhd/dot_general | solution.py:111
  566.2 14.7 %fusion.150 = bf16[8,4,32,64]{3,2,1,0:T(8,128)(2,1)S(1)} fusion(bf16[8,192,4,32]{1,3,2,0:T(8,128)(2,1)S(1)} %bitcast.159, f32[8,4,64,192]{3,2,1,0:T(8,128)} %copy-done.4, f32[8,4,64,192]{3,2,1,0:T(8,128)} %copy-done.3, f32[8,4,64]{2,1,0:T(4,128)S(1)} %get-tuple-element.229), kind=kOutput, calls=%fused_computation.26.clone.1 | convolution fusion | flops 27920576 | bytes 3678208 | tf_op jit(solution)/shard_map/while/body/eval_jaxpr/nhqk,nkhd->nqhd/dot_general | solution.py:108
  595.5 14.5 %fusion.151 = f32[8,192,4,32]{1,3,2,0:T(8,128)} fusion(bf16[8,64,4,32]{1,3,2,0:T(8,128)(2,1)} %bitcast.165, f32[8,4,64,192]{3,2,1,0:T(8,128)S(1)} %fusion.148, f32[8,4,64,192]{3,2,1,0:T(8,128)} %copy-done.3, f32[8,4,64]{2,1,0:T(4,128)S(1)} %get-tuple-element.229), kind=kOutput, calls=%fused_computation.29.clone.1 | convolution fusion | flops 27920576 | bytes 4071424 | tf_op jit(solution)/shard_map/while/body/eval_jaxpr/nhqk,nqhd->nkhd/dot_general | solution.py:111
  616.8 14.7 %fusion.150 = bf16[8,4,32,64]{3,2,1,0:T(8,128)(2,1)S(1)} fusion(bf16[8,192,4,32]{1,3,2,0:T(8,128)(2,1)S(1)} %bitcast.159, f32[8,4,64,192]{3,2,1,0:T(8,128)} %copy-done.4, f32[8,4,64,192]{3,2,1,0:T(8,128)} %copy-done.3, f32[8,4,64]{2,1,0:T(4,128)S(1)} %get-tuple-element.229), kind=kOutput, calls=%fused_computation.26.clone.1 | convolution fusion | flops 27920576 | bytes 3678208 | tf_op jit(solution)/shard_map/while/body/eval_jaxpr/nhqk,nkhd->nqhd/dot_general | solution.py:108
  646.1 14.5 %fusion.151 = f32[8,192,4,32]{1,3,2,0:T(8,128)} fusion(bf16[8,64,4,32]{1,3,2,0:T(8,128)(2,1)} %bitcast.165, f32[8,4,64,192]{3,2,1,0:T(8,128)S(1)} %fusion.148, f32[8,4,64,192]{3,2,1,0:T(8,128)} %copy-done.3, f32[8,4,64]{2,1,0:T(4,128)S(1)} %get-tuple-element.229), kind=kOutput, calls=%fused_computation.29.clone.1 | convolution fusion | flops 27920576 | bytes 4071424 | tf_op jit(solution)/shard_map/while/body/eval_jaxpr/nhqk,nqhd->nkhd/dot_general | solution.py:111
  667.3 14.7 %fusion.150 = bf16[8,4,32,64]{3,2,1,0:T(8,128)(2,1)S(1)} fusion(bf16[8,192,4,32]{1,3,2,0:T(8,128)(2,1)S(1)} %bitcast.159, f32[8,4,64,192]{3,2,1,0:T(8,128)} %copy-done.4, f32[8,4,64,192]{3,2,1,0:T(8,128)} %copy-done.3, f32[8,4,64]{2,1,0:T(4,128)S(1)} %get-tuple-element.229), kind=kOutput, calls=%fused_computation.26.clone.1 | convolution fusion | flops 27920576 | bytes 3678208 | tf_op jit(solution)/shard_map/while/body/eval_jaxpr/nhqk,nkhd->nqhd/dot_general | solution.py:108
  696.6 14.5 %fusion.151 = f32[8,192,4,32]{1,3,2,0:T(8,128)} fusion(bf16[8,64,4,32]{1,3,2,0:T(8,128)(2,1)} %bitcast.165, f32[8,4,64,192]{3,2,1,0:T(8,128)S(1)} %fusion.148, f32[8,4,64,192]{3,2,1,0:T(8,128)} %copy-done.3, f32[8,4,64]{2,1,0:T(4,128)S(1)} %get-tuple-element.229), kind=kOutput, calls=%fused_computation.29.clone.1 | convolution fusion | flops 27920576 | bytes 4071424 | tf_op jit(solution)/shard_map/while/body/eval_jaxpr/nhqk,nqhd->nkhd/dot_general | solution.py:111
  717.8 14.7 %fusion.150 = bf16[8,4,32,64]{3,2,1,0:T(8,128)(2,1)S(1)} fusion(bf16[8,192,4,32]{1,3,2,0:T(8,128)(2,1)S(1)} %bitcast.159, f32[8,4,64,192]{3,2,1,0:T(8,128)} %copy-done.4, f32[8,4,64,192]{3,2,1,0:T(8,128)} %copy-done.3, f32[8,4,64]{2,1,0:T(4,128)S(1)} %get-tuple-element.229), kind=kOutput, calls=%fused_computation.26.clone.1 | convolution fusion | flops 27920576 | bytes 3678208 | tf_op jit(solution)/shard_map/while/body/eval_jaxpr/nhqk,nkhd->nqhd/dot_general | solution.py:108
  737.6 19.3 %scatter_fusion = bf16[256,64,256]{2,1,0:T(8,128)(2,1)} fusion(bf16[256,64,256]{2,1,0:T(8,128)(2,1)} %broadcast_in_dim.60, s32[128]{0:T(128)S(1)} %copy-done.37, bf16[128,64,256]{2,1,0:T(8,128)(2,1)} %bitcast.180), kind=kCustom, calls=%fused_computation.3 | custom fusion | bytes 12583424 | tf_op jit(solution)/shard_map/scatter | solution.py:221
  757.1 13.4 %collective-permute-done.2 = bf16[16,16,64,256]{3,2,1,0:T(8,128)(2,1)} collective-permute-done((bf16[16,16,64,256]{3,2,1,0:T(8,128)(2,1)}, bf16[16,16,64,256]{3,2,1,0:T(8,128)(2,1)}, u32[]{:S(2)}, u32[]{:S(2)}) %collective-permute-start.2) | collective-permute-done | bytes 8388640 | tf_op jit(solution)/shard_map/ppermute | solution.py:19
  777.8 6.1 fusion.70
  788.2 146.4 %all-to-all-done.2 = bf16[16,16,64,256]{3,2,1,0:T(8,128)(2,1)} async-done(((bf16[16,16,64,256]{3,2,1,0:T(8,128)(2,1)}), bf16[16,16,64,256]{3,2,1,0:T(8,128)(2,1)}, u32[]{:S(2)}, u32[]{:S(2)}) %all-to-all-start.2) | async-done | bytes 8388640 | tf_op jit(solution)/shard_map/all_to_all | solution.py:152
  934.6 11.3 bitcast_convert_fusion
  945.8 49.5 %scatter_fusion.1 = f32[64,64,256]{2,1,0:T(8,128)} fusion(f32[64,64,256]{2,1,0:T(8,128)} %bitcast.157, s32[256]{0:T(256)S(1)} %bitcast.189, f32[256,64,256]{2,1,0:T(8,128)} %bitcast_convert_fusion), kind=kCustom, calls=%fused_computation.4 | custom fusion | flops 4194304 | bytes 50332672 | tf_op jit(solution)/shard_map/scatter-add | solution.py:226
  1010.5 158.0 %all-reduce.3.cloned.1.call-done = (f32[128,384]{1,0:T(8,128)}, f32[128,128]{1,0:T(8,128)}, f32[128,512]{1,0:T(8,128)}, f32[512,128]{1,0:T(8,128)}) async-done(((f32[128,384]{1,0:T(8,128)}, f32[128,128]{1,0:T(8,128)}, f32[128,512]{1,0:T(8,128)}, f32[512,128]{1,0:T(8,128)}), (f32[128,384]{1,0:T(8,128)}, f32[128,128]{1,0:T(8,128)}, f32[128,512]{1,0:T(8,128)}, ...) | async-done | bytes 786448 | tf_op jit(solution)/shard_map/psum | solution.py:234
  (400 shorter events, 290.4 us)
Async XLA Ops:
  7.2 302.6 %copy-start = (bf16[128,512]{1,0:T(8,128)(2,1)S(1)}, bf16[128,512]{1,0:T(8,128)(2,1)}, u32[]{:S(2)}) copy-start(bf16[128,512]{1,0:T(8,128)(2,1)} %param.17) | copy-start | bytes 393220
  7.2 6.7 copy-start.10
  10.5 225.1 %copy-start.36 = (s32[128]{0:T(128)}, s32[128]{0:T(128)S(1)}, u32[]{:S(2)}) copy-start(s32[128]{0:T(128)S(1)} %fusion.65) | copy-start | bytes 1540
  11.6 5.1 copy-start.32
  11.6 7.7 collective-permute-start
  15.3 4.0 copy-start.23
  15.4 3.9 copy-start.25
  16.6 2.6 copy-start.14
  19.3 15.2 %all-to-all-start = ((s32[16,1,16]{2,1,0:T(1,128)}), s32[16,1,16]{2,1,0:T(1,128)S(1)}, u32[]{:S(2)}, u32[]{:S(2)}) async-start(s32[16,1,16]{2,1,0:T(1,128)} %bitcast.22), calls=%async_computation | async-start | bytes 16384 | tf_op jit(solution)/shard_map/all_to_all | solution.py:187
  34.5 9.7 copy-start.34
  232.4 13.5 %collective-permute-start.1 = (bf16[16,16,64,256]{3,2,1,0:T(8,128)(2,1)}, bf16[16,16,64,256]{3,2,1,0:T(8,128)(2,1)}, u32[]{:S(2)}, u32[]{:S(2)}) collective-permute-start(bf16[16,16,64,256]{3,2,1,0:T(8,128)(2,1)} %all_to_all.19), channel_id=1, source_target_pairs={{0,16},{16,0},{1,17},{17,1},{2,18},{18,2},{3,19},{19,3},{4,20},{20... | collective-permute-start | bytes 25165832 | tf_op jit(solution)/shard_map/ppermute | solution.py:19
  245.9 6.3 copy-start.16
  308.1 15.3 %copy-start.5 = (bf16[4096,128]{1,0:T(8,128)(2,1)}, bf16[4096,128]{1,0:T(8,128)(2,1)S(1)}, u32[]{:S(2)}) copy-start(bf16[4096,128]{1,0:T(8,128)(2,1)S(1)} %fusion.45) | copy-start | bytes 3145732
  308.5 14.9 %copy-start.21 = (f32[4096]{0:T(1024)}, f32[4096]{0:T(1024)S(1)}, u32[]{:S(2)}) copy-start(f32[4096]{0:T(1024)S(1)} %broadcast_multiply_fusion.9) | copy-start | bytes 49156
  309.8 13.6 %copy-start.27 = (f32[4096]{0:T(1024)}, f32[4096]{0:T(1024)S(1)}, u32[]{:S(2)}) copy-start(f32[4096]{0:T(1024)S(1)} %add_rsqrt_fusion.1) | copy-start | bytes 49156
  309.8 5.5 copy-start.18
  309.8 5.5 copy-start.29
  323.4 3.9 copy-start.31
  733.3 4.3 copy-start.37
  756.9 18.3 %copy-start.35 = (s32[16,1,16]{2,1,0:T(1,128)S(1)}, s32[16,1,16]{2,1,0:T(1,128)}, u32[]{:S(2)}) copy-start(s32[16,1,16]{2,1,0:T(1,128)} %copy-done.34) | copy-start | bytes 3076
  756.9 18.4 %copy-start.8 = (f32[4096,128]{1,0:T(8,128)S(1)}, f32[4096,128]{1,0:T(8,128)}, u32[]{:S(2)}) copy-start(f32[4096,128]{1,0:T(8,128)} %copy-done.7) | copy-start | bytes 6291460
  756.9 13.5 %collective-permute-start.2 = (bf16[16,16,64,256]{3,2,1,0:T(8,128)(2,1)}, bf16[16,16,64,256]{3,2,1,0:T(8,128)(2,1)}, u32[]{:S(2)}, u32[]{:S(2)}) collective-permute-start(bf16[16,16,64,256]{3,2,1,0:T(8,128)(2,1)} %bitcast.172), channel_id=1, source_target_pairs={{0,16},{16,0},{1,17},{17,1},{2,18},{18,2},{3,19},{19,3},{4,20},{20... | collective-permute-start | bytes 25165832 | tf_op jit(solution)/shard_map/ppermute | solution.py:19
  770.4 164.1 %all-to-all-start.2 = ((bf16[16,16,64,256]{3,2,1,0:T(8,128)(2,1)}), bf16[16,16,64,256]{3,2,1,0:T(8,128)(2,1)}, u32[]{:S(2)}, u32[]{:S(2)}) async-start(bf16[16,16,64,256]{3,2,1,0:T(8,128)(2,1)} %collective-permute-done.2), calls=%async_computation.2 | async-start | bytes 16777216 | tf_op jit(solution)/shard_map/all_to_all | solution.py:152
  775.2 2.6 copy-start.6
  775.2 2.6 copy-start.22
  775.2 2.6 copy-start.28
  775.2 393.2 %all-reduce.3.cloned.1.call-start = ((), (), s32[]{:S(2)}) async-start(), calls=%async_computation.3 | async-start | bytes 1572864 | tf_op jit(solution)/shard_map/psum | solution.py:234
  777.8 6.1 copy-start.9
  777.8 6.1 copy-start.19
  995.4 4.0 copy-start.15
  995.4 4.0 copy-start.38
  1005.6 169.2 %copy-start.1 = (bf16[128,512]{1,0:T(8,128)(2,1)S(1)}, bf16[128,512]{1,0:T(8,128)(2,1)}, u32[]{:S(2)}) copy-start(bf16[128,512]{1,0:T(8,128)(2,1)} %param.17) | copy-start | bytes 393220
  (48 other events, 74.5 us)
Sparse Core Ops, SparseCore 0:
  1005.8 162.6 all-reduce.2
where the time goes:
time: 1190 us; the launch traced here: 1180 us
  waiting for transfers between devices  332 us (28%)
  matrix products  318 us (27%)
  local copies, waits for them, and re-layouts  202 us (17%)
  blocking collectives  188 us (16%)
  other arithmetic  113 us (9%)
  between operations  15 us (1%)
  starting transfers between devices  13.3 us (1%)
    all_to_all x1, blocking collectives, deliver(): lax.all_to_all(parcel, ('grp', 'sp'), split_axis=0, concat_axis=0, tiled=...  188 us
    psum x1, waiting for transfers between devices, body(): lax.psum((qkv_part, grads[0], grads[1], grads[2]), ('pair', 'grp', 'sp'))  158 us
    all_to_all x1, waiting for transfers between devices, deliver(): lax.all_to_all(parcel, ('grp', 'sp'), split_axis=0, concat_axis=0, tiled=...  146 us
    dot_general x8, matrix products, attend_back(): jnp.einsum('nhqk,nkhd->nqhd', grad_scores, head_keys, preferred_element_t...  117 us
    dot_general x8, matrix products, attend_back(): jnp.einsum('nhqk,nqhd->nkhd', grad_scores, head_query, preferred_element_...  116 us
    concatenate x32, local copies, waits for them, and re-layouts, attend_back(): jnp.concatenate([grad_keys, grad_values], axis=-1)  55.9 us
    scatter-add x1, other arithmetic, body(): kv_grad = self_grad.at[wanted_flat].add(returned_up, mode='drop')  49.5 us
    dynamic_slice x32, local copies, waits for them, and re-layouts, body(): lax.map(forward_group, (query_groups, kv_groups)).reshape(rows_total, width)  25.5 us
  transfers between devices with their start and end apart: 6, of which 5 were waited for; matrix products, arithmetic and copies ran while one was open for 3% of the time, Pallas kernels for 0%

commit v1 on v0

v1 whole, which is shorter than its diff:
```python
import functools
import math

import jax
import jax.numpy as jnp
from jax import lax
from jax.experimental import pallas as pl
from jax.experimental.pallas import tpu as pltpu
from jax.sharding import PartitionSpec as P

HEADS = 4
GROUP_SIZE = 4
VMEM_LIMIT = 60 * 1024 * 1024


eps_norm = 1e-05
gelu_scale = 0.7978845608028654
gelu_cubic = 0.044715


def norm_rows(values):
    centred = values - jnp.mean(values, axis=-1, keepdims=True)
    factor = lax.rsqrt(jnp.mean(centred * centred, axis=-1, keepdims=True) + eps_norm)
    return (centred * factor, factor)


def norm_back(upstream, normed, factor):
    return factor * (
        upstream
        - jnp.mean(upstream, axis=-1, keepdims=True)
        - normed * jnp.mean(upstream * normed, axis=-1, keepdims=True)
    )


def gelu_pair(upper):
    squared = upper * upper
    tangent = jnp.tanh(gelu_scale * upper * (1.0 + gelu_cubic * squared))
    half = 0.5 * (1.0 + tangent)
    value = upper * half
    slope = half + 0.5 * upper * (1.0 - tangent * tangent) * (
        gelu_scale + (3.0 * gelu_cubic * gelu_scale) * squared
    )
    return (value, slope)


def matmul(former, latter):
    return jnp.dot(former, latter, preferred_element_type=jnp.float32)


def against(former, latter):
    return lax.dot_general(
        former, latter, (((1,), (1,)), ((), ())), preferred_element_type=jnp.float32
    )


def outer_sum(former, latter):
    return lax.dot_general(
        former, latter, (((0,), (0,)), ((), ())), preferred_element_type=jnp.float32
    )


def head_mask(window_len, width):
    row_head = lax.broadcasted_iota(jnp.int32, (HEADS * window_len, width), 0) // window_len
    col_head = lax.broadcasted_iota(jnp.int32, (HEADS * window_len, width), 1) // (width // HEADS)
    return jnp.where(row_head == col_head, 1.0, 0.0).astype(jnp.bfloat16)


def spread_heads(rows, mask):
    return jnp.concatenate([rows] * HEADS, axis=0) * mask


def gather_heads(full, window_len):
    width = full.shape[-1]
    lane = lax.broadcasted_iota(jnp.int32, (window_len, width), 1) // (width // HEADS)
    result = full[:window_len]
    for head in range(1, HEADS):
        result = jnp.where(lane == head, full[head * window_len : (head + 1) * window_len], result)
    return result


def pick_kernel(wanted, tokens, picked, normed):
    windows, window_len, width = tokens.shape

    @pl.loop(0, windows // 4)
    def _(step):
        rows = tokens[pl.ds(step * 4, 4)].astype(jnp.float32)
        normed[pl.ds(step * 4, 4)] = norm_rows(rows)[0].astype(jnp.bfloat16)

    @pl.loop(0, picked.shape[0] // 8)
    def _(step):
        for inner in range(8):
            slot = step * 8 + inner
            window = jnp.clip(wanted[slot], 0, windows - 1)
            picked[slot] = normed[window]


def main_kernel(
    position,
    tokens,
    cotangent,
    answered,
    weight_qkv,
    weight_out,
    weight_up,
    weight_down,
    block_out,
    grad_resid_out,
    grad_query_out,
    self_grad,
    outbound,
    weight_grads,
    weights_buf,
    kv_buf,
    query_buf,
    mixed_buf,
):
    step = pl.program_id(0)
    window_len = answered.shape[1]
    width = tokens.shape[-1]
    group = tokens.shape[0] // window_len
    fanout = kv_buf.shape[1] // window_len - 1
    factor = 1.0 / math.sqrt(width // HEADS)
    mask = head_mask(window_len, width)

    @pl.when(step == 0)
    def _():
        weight_grads[...] = jnp.zeros_like(weight_grads)

    rows = tokens[...].astype(jnp.float32)
    normed1_low = norm_rows(rows)[0].astype(jnp.bfloat16)
    qkv = matmul(normed1_low, weight_qkv[...]).astype(jnp.bfloat16)
    for item in range(group):
        own = slice(item * window_len, (item + 1) * window_len)
        far = jnp.concatenate(
            [answered[position[(step * group + item) * fanout + j]] for j in range(fanout)], axis=0
        )
        far_kv = matmul(far, weight_qkv[:, width:]).astype(jnp.bfloat16)
        kv = jnp.concatenate([qkv[own, width:], far_kv], axis=0)
        kv_buf[item] = kv
        query = spread_heads(qkv[own, :width], mask)
        query_buf[item] = query
        scores = against(kv[:, :width], query)
        peak = jnp.max(scores, axis=0, keepdims=True)
        powers = jnp.exp((scores - peak) * factor)
        weights = powers * (1.0 / jnp.sum(powers, axis=0, keepdims=True))
        weights_buf[item] = weights
        full = outer_sum(weights.astype(jnp.bfloat16), kv[:, width:])
        mixed_buf[own] = gather_heads(full, window_len).astype(jnp.bfloat16)

    mixed = mixed_buf[...]
    cot = cotangent[...]
    resid = (rows + matmul(mixed, weight_out[...])).astype(jnp.bfloat16).astype(jnp.float32)
    normed2, factor2 = norm_rows(resid)
    normed2_low = normed2.astype(jnp.bfloat16)
    value, slope = gelu_pair(matmul(normed2_low, weight_up[...]))
    act = value.astype(jnp.bfloat16)
    block_out[...] = (resid + matmul(act, weight_down[...])).astype(jnp.bfloat16)
    grad_upper = (against(cot, weight_down[...]) * slope).astype(jnp.bfloat16)
    grad_resid = cot.astype(jnp.float32) + norm_back(
        against(grad_upper, weight_up[...]), normed2, factor2
    )
    grad_resid_out[...] = grad_resid
    grad_resid_low = grad_resid.astype(jnp.bfloat16)
    grad_mixed = against(grad_resid_low, weight_out[...]).astype(jnp.bfloat16)
    grad_out = outer_sum(mixed, grad_resid_low)
    grad_up = outer_sum(normed2_low, grad_upper)
    grad_down = outer_sum(act, cot)
    blocks = grad_upper.shape[-1] // width
    weight_grads[:width] += grad_out
    for block in range(blocks):
        weight_grads[(1 + block) * width : (2 + block) * width] += grad_up[
            :, block * width : (block + 1) * width
        ]
    weight_grads[(1 + blocks) * width :] += grad_down

    for item in range(group):
        own = slice(item * window_len, (item + 1) * window_len)
        kv = kv_buf[item]
        query = query_buf[item]
        weights = weights_buf[item]
        head_grad = spread_heads(grad_mixed[own], mask)
        grad_weights = against(kv[:, width:], head_grad)
        inner = jnp.sum(grad_weights * weights, axis=0, keepdims=True)
        grad_scores = (weights * (grad_weights - inner) * factor).astype(jnp.bfloat16)
        full = outer_sum(grad_scores, kv[:, :width])
        grad_query_out[own] = gather_heads(full, window_len).astype(jnp.bfloat16)
        grad_keys = matmul(grad_scores, query)
        grad_values = matmul(weights.astype(jnp.bfloat16), head_grad)
        self_grad[own, :width] = grad_keys[:window_len]
        self_grad[own, width:] = grad_values[:window_len]
        for j in range(fanout):
            slot = position[(step * group + item) * fanout + j]
            source = slice((j + 1) * window_len, (j + 2) * window_len)
            outbound[slot, :, :width] = grad_keys[source].astype(jnp.bfloat16)
            outbound[slot, :, width:] = grad_values[source].astype(jnp.bfloat16)


def last_kernel(
    wanted, returned, self_grad, grad_query, grad_resid, tokens, weight_qkv, grad_tokens, weight_grads, total
):
    step = pl.program_id(0)
    windows, window_len, width = tokens.shape
    slots = returned.shape[0]

    @pl.when(step == 0)
    def _():
        total[...] = self_grad[...]
        weight_grads[...] = jnp.zeros_like(weight_grads)

    for slot in range(slots):
        window = wanted[step * slots + slot]

        @pl.when(window < windows)
        def _():
            total[window] += returned[slot].astype(jnp.float32)

    @pl.when(step == pl.num_programs(0) - 1)
    def _():
        @pl.loop(0, windows // GROUP_SIZE)
        def _(part):
            span = pl.ds(part * GROUP_SIZE, GROUP_SIZE)
            count = GROUP_SIZE * window_len
            normed1, factor1 = norm_rows(tokens[span].reshape(count, width).astype(jnp.float32))
            grads = jnp.concatenate(
                [
                    grad_query[span].reshape(count, width),
                    total[span].reshape(count, 2 * width).astype(jnp.bfloat16),
                ],
                axis=1,
            )
            upstream = against(grads, weight_qkv[...])
            result = grad_resid[span].reshape(count, width) + norm_back(upstream, normed1, factor1)
            grad_tokens[span] = result.astype(jnp.bfloat16).reshape(GROUP_SIZE, window_len, width)
            sums = outer_sum(normed1.astype(jnp.bfloat16), grads)
            for block in range(3):
                weight_grads[block * width : (block + 1) * width] += sums[
                    :, block * width : (block + 1) * width
                ]


def swapped(value):
    return lax.ppermute(value, "pair", [(0, 1), (1, 0)])


def deliver(parcel):
    return lax.all_to_all(parcel, ("grp", "sp"), split_axis=0, concat_axis=0, tiled=True)


ALL = ("pair", "grp", "sp")


def summed(rows):
    devices = lax.axis_size(ALL)
    share = lax.all_to_all(
        rows.reshape(devices, rows.shape[0] // devices, rows.shape[1]),
        ALL,
        split_axis=0,
        concat_axis=0,
        tiled=True,
    )
    copies = jnp.broadcast_to(jnp.sum(share, axis=0)[None], share.shape)
    copies = lax.all_to_all(copies, ALL, split_axis=0, concat_axis=0, tiled=True)
    return copies.reshape(rows.shape)


def whole(shape):
    return pl.BlockSpec(shape, lambda *_: (0,) * len(shape))


def body(tokens, owner_ids, local_ids, weight_qkv, weight_out, weight_up, weight_down, cotangent):
    holders = lax.axis_size("grp") * lax.axis_size("sp")
    width = tokens.shape[-1]
    hidden = weight_up.shape[-1]
    windows = tokens.shape[1]
    window_len = tokens.shape[2]
    fanout = owner_ids.shape[-1]
    slots = max(2, 2 * windows * fanout // holders)
    keys_len = (fanout + 1) * window_len
    rows_total = windows * window_len
    group = GROUP_SIZE
    group_rows = group * window_len
    token_rows = tokens[0].reshape(rows_total, width)
    cot_rows = cotangent[0].reshape(rows_total, width)
    params = pltpu.CompilerParams(vmem_limit_bytes=VMEM_LIMIT)

    owners = owner_ids[0].reshape(-1)
    local_rows = local_ids[0].reshape(-1)
    onehot = (owners[:, None] == jnp.arange(holders, dtype=jnp.int32)[None, :]).astype(jnp.int32)
    ranks = jnp.sum((jnp.cumsum(onehot, axis=0) - 1) * onehot, axis=1)
    position = owners * slots + ranks
    requests = (
        jnp.full((holders * slots,), windows, jnp.int32)
        .at[position]
        .set(local_rows)
        .reshape(holders, slots)
    )
    wanted_flat = deliver(swapped(requests)).reshape(-1)

    picked = pl.pallas_call(
        pick_kernel,
        grid_spec=pltpu.PrefetchScalarGridSpec(
            num_scalar_prefetch=1,
            grid=(1,),
            in_specs=[whole((windows, window_len, width))],
            out_specs=whole((holders * slots, window_len, width)),
            scratch_shapes=[pltpu.VMEM((windows, window_len, width), jnp.bfloat16)],
        ),
        out_shape=jax.ShapeDtypeStruct((holders * slots, window_len, width), jnp.bfloat16),
        compiler_params=params,
        name="pick",
    )(wanted_flat, tokens[0])
    answered = swapped(deliver(picked.reshape(holders, slots, window_len, width)))
    answered = answered.reshape(holders * slots, window_len, width)

    blocks = hidden // width
    row_spec = pl.BlockSpec((group_rows, width), lambda i, *_: (i, 0))
    out_rows, grad_resid, grad_query, self_grad, outbound, tail_grads = pl.pallas_call(
        main_kernel,
        grid_spec=pltpu.PrefetchScalarGridSpec(
            num_scalar_prefetch=1,
            grid=(windows // group,),
            in_specs=[
                row_spec,
                row_spec,
                whole((holders * slots, window_len, width)),
                whole((width, 3 * width)),
                whole((width, width)),
                whole((width, hidden)),
                whole((hidden, width)),
            ],
            out_specs=[
                row_spec,
                row_spec,
                row_spec,
                pl.BlockSpec((group_rows, 2 * width), lambda i, *_: (i, 0)),
                whole((holders * slots, window_len, 2 * width)),
                whole(((1 + 2 * blocks) * width, width)),
            ],
            scratch_shapes=[
                pltpu.VMEM((group, keys_len, HEADS * window_len), jnp.float32),
                pltpu.VMEM((group, keys_len, 2 * width), jnp.bfloat16),
                pltpu.VMEM((group, HEADS * window_len, width), jnp.bfloat16),
                pltpu.VMEM((group_rows, width), jnp.bfloat16),
            ],
        ),
        out_shape=[
            jax.ShapeDtypeStruct((rows_total, width), jnp.bfloat16),
            jax.ShapeDtypeStruct((rows_total, width), jnp.float32),
            jax.ShapeDtypeStruct((rows_total, width), jnp.bfloat16),
            jax.ShapeDtypeStruct((rows_total, 2 * width), jnp.float32),
            jax.ShapeDtypeStruct((holders * slots, window_len, 2 * width), jnp.bfloat16),
            jax.ShapeDtypeStruct(((1 + 2 * blocks) * width, width), jnp.float32),
        ],
        compiler_params=params,
        name="attend_and_tail",
    )(position, token_rows, cot_rows, answered, weight_qkv, weight_out, weight_up, weight_down)

    returned = deliver(swapped(outbound.reshape(holders, slots, window_len, 2 * width)))
    returned = returned.reshape(holders * slots, window_len, 2 * width)

    grad_rows, qkv_grads = pl.pallas_call(
        last_kernel,
        grid_spec=pltpu.PrefetchScalarGridSpec(
            num_scalar_prefetch=1,
            grid=(holders,),
            in_specs=[
                pl.BlockSpec((slots, window_len, 2 * width), lambda i, *_: (i, 0, 0)),
                whole((windows, window_len, 2 * width)),
                whole((windows, window_len, width)),
                whole((windows, window_len, width)),
                whole((windows, window_len, width)),
                whole((width, 3 * width)),
            ],
            out_specs=[
                whole((windows, window_len, width)),
                whole((3 * width, width)),
            ],
            scratch_shapes=[pltpu.VMEM((windows, window_len, 2 * width), jnp.float32)],
        ),
        out_shape=[
            jax.ShapeDtypeStruct((windows, window_len, width), jnp.bfloat16),
            jax.ShapeDtypeStruct((3 * width, width), jnp.float32),
        ],
        compiler_params=params,
        name="collect",
    )(
        wanted_flat,
        returned,
        self_grad.reshape(windows, window_len, 2 * width),
        grad_query.reshape(windows, window_len, width),
        grad_resid.reshape(windows, window_len, width),
        tokens[0],
        weight_qkv,
    )

    inv_count = 1.0 / math.sqrt(2 * windows * holders * window_len)
    totals = summed(jnp.concatenate([qkv_grads, tail_grads], axis=0)) * inv_count
    sums = totals.reshape(4 + 2 * blocks, width, width)

    def wide(first, count):
        return sums[first : first + count].transpose(1, 0, 2).reshape(width, count * width)

    return (
        out_rows.reshape(1, windows, window_len, width),
        grad_rows[None],
        wide(0, 3),
        sums[3],
        wide(4, blocks),
        sums[4 + blocks :].reshape(hidden, width),
    )


def solution(mesh):
    in_specs = (
        P("pair", ("grp", "sp"), None, None),
        P("pair", ("grp", "sp"), None),
        P("pair", ("grp", "sp"), None),
        P(),
        P(),
        P(),
        P(),
        P("pair", ("grp", "sp"), None, None),
    )
    out_specs = (
        P("pair", ("grp", "sp"), None, None),
        P("pair", ("grp", "sp"), None, None),
        P(),
        P(),
        P(),
        P(),
    )
    return jax.shard_map(body, mesh=mesh, in_specs=in_specs, out_specs=out_specs, check_vma=False)
```

time: 1190 us -> 489 us (0.41)
  matrix products: 318 us -> 0 us
  waiting for transfers between devices: 332 us -> 20.8 us
  local copies, waits for them, and re-layouts: 202 us -> 7.37 us
  blocking collectives: 188 us -> 349 us
  other arithmetic: 113 us -> 3.41 us
  Pallas kernels: 0 us -> 106 us
  between operations: 15 us -> 0.71 us
  starting transfers between devices: 13.3 us -> 0.67 us
    dot_general x52 -> x0, matrix products: 301 us -> none  [the longest x8 117 us: attend_back(): jnp.einsum('nhqk,nkhd->nqhd', grad_scores, head_keys, preferred_element_t...]
    psum x1 -> x0, waiting for transfers between devices: 158 us -> none  [body(): lax.psum((qkv_part, grads[0], grads[1], grads[2]), ('pair', 'grp', 'sp'))]
    all_to_all x2 -> x0, waiting for transfers between devices: 150 us -> none  [the longest x1 146 us: deliver(): lax.all_to_all(parcel, ('grp', 'sp'), split_axis=0, concat_axis=0, tiled=...]
    all_to_all x1 -> x3, blocking collectives: 188 us -> 300 us  [deliver(): lax.all_to_all(parcel, ('grp', 'sp'), split_axis=0, concat_axis=0, tiled=...]
    pallas_call x0 -> x3, Pallas kernels: none -> 106 us  [the longest x1 76.2 us: body(): pl.pallas_call(main_kernel, grid_spec=pltpu.PrefetchScalarGridSpec(num_sc...]
    concatenate x32 -> x0, local copies, waits for them, and re-layouts: 55.9 us -> none  [attend_back(): jnp.concatenate([grad_keys, grad_values], axis=-1)]
    scatter-add x1 -> x0, other arithmetic: 49.5 us -> none  [body(): kv_grad = self_grad.at[wanted_flat].add(returned_up, mode='drop')]
    all_to_all x0 -> x2, blocking collectives: none -> 49.4 us  [the longest x1 25.2 us: summed(): lax.all_to_all(rows.reshape(devices, rows.shape[0] // devices, rows.shape...]
  transfers between devices with their start and end apart: 6 -> 3, of which waited for: 5 -> 3; matrix products, arithmetic and copies ran while one was open for 3% -> 0% of each run, Pallas kernels for 0% -> 0%
where the time goes in v1:
time: 489 us; the launch traced here: 488 us
  blocking collectives  349 us (71%)
  Pallas kernels  106 us (22%)
  waiting for transfers between devices  20.8 us (4%)
  local copies, waits for them, and re-layouts  7.37 us (2%)
    all_to_all x3, blocking collectives, deliver(): lax.all_to_all(parcel, ('grp', 'sp'), split_axis=0, concat_axis=0, tiled=...  300 us
    pallas_call x1, Pallas kernels, body(): pl.pallas_call(main_kernel, grid_spec=pltpu.PrefetchScalarGridSpec(num_sc...  76.2 us
    all_to_all x1, blocking collectives, summed(): lax.all_to_all(rows.reshape(devices, rows.shape[0] // devices, rows.shape...  25.2 us
    all_to_all x1, blocking collectives, summed(): lax.all_to_all(copies, ALL, split_axis=0, concat_axis=0, tiled=True)  24.2 us
    pallas_call x1, Pallas kernels, body(): pl.pallas_call(last_kernel, grid_spec=pltpu.PrefetchScalarGridSpec(num_sc...  21.8 us
    ppermute x3, waiting for transfers between devices, swapped(): return lax.ppermute(value, 'pair', [(0, 1), (1, 0)])  20.8 us
  transfers between devices with their start and end apart: 3, of which 3 were waited for; matrix products, arithmetic and copies ran while one was open for 0% of the time, Pallas kernels for 0%

profile of v1, /device:TPU:0, one launch (start us, length us, event | category | flops | bytes accessed | tf_op | source)
XLA Modules:
  0.0 488.1 jit_solution(12445365036841700120)
XLA Ops:
  0.6 0.7 broadcast_multiply_fusion.1
  1.3 0.8 copy.30
  2.2 0.1 mul.37
  2.3 0.8 copy.32
  3.1 0.1 reshape.114
  3.2 0.1 reshape_squeeze.12
  3.5 0.2 reduce_window_sum.11
  3.6 0.2 select_reduce_fusion
  3.8 1.0 scatter_custom_fusion
  4.9 0.5 collective-permute-start
  5.4 0.8 collective-permute-done
  6.2 15.3 %all_to_all.29 = s32[16,1,16]{2,1,0:T(1,128)S(1)} all-to-all(s32[16,1,16]{2,1,0:T(1,128)S(1)} %bitcast.49), channel_id=1, replica_groups=mesh['pair'=2,'grp'=4,'sp'=4] {'grp','sp'}, dimensions={0} | all-to-all | bytes 2048 | tf_op jit(solution)/shard_map/all_to_all | solution.py:246
  21.4 0.5 broadcast.39
  22.0 0.7 reduce.3
  22.6 0.6 reshape.98.wanted
  23.3 7.8 %pick.1 = bf16[256,64,128]{2,1,0:T(8,128)(2,1)} custom-call(s32[256]{0:T(256)} %reshape.98.wanted, bf16[64,64,128]{2,1,0:T(8,128)(2,1)} %bitcast.35), custom_call_target="tpu_custom_call" | custom-call | tf_op jit(solution)/shard_map/pick/pallas_call | solution.py:299
  31.1 96.9 %all_to_all.30 = bf16[16,16,64,128]{3,2,1,0:T(8,128)(2,1)S(1)} all-to-all(bf16[16,16,64,128]{3,2,1,0:T(8,128)(2,1)} %bitcast.34), channel_id=1, replica_groups=mesh['pair'=2,'grp'=4,'sp'=4] {'grp','sp'}, dimensions={0} | all-to-all | bytes 8388608 | tf_op jit(solution)/shard_map/all_to_all | solution.py:246
  127.9 0.5 multiply_add_fusion.position
  128.5 6.8 %collective-permute-done.1 = bf16[16,16,64,128]{3,2,1,0:T(8,128)(2,1)} collective-permute-done((bf16[16,16,64,128]{3,2,1,0:T(8,128)(2,1)S(1)}, bf16[16,16,64,128]{3,2,1,0:T(8,128)(2,1)}, u32[]{:S(2)}, u32[]{:S(2)}) %collective-permute-start.1) | collective-permute-done | bytes 4194336 | tf_op jit(solution)/shard_map/ppermute | solution.py:242
  135.2 76.2 %attend_and_tail.1 = (bf16[4096,128]{1,0:T(8,128)(2,1)}, f32[4096,128]{1,0:T(8,128)}, bf16[4096,128]{1,0:T(8,128)(2,1)}, f32[4096,256]{1,0:T(8,128)}, bf16[256,6...) custom-call(s32[128]{0:T(128)} %multiply_add_fusion.position, bf16[4096,128]{1,0:T(8,128)(2,1)} %bitcast.36, ...), custom_call_target="tpu_custom_call" | custom-call | tf_op jit(solution)/shard_map/attend_and_tail/pallas_call | solution.py:317
  211.4 0.2 collective-permute-start.2
  211.6 13.2 %collective-permute-done.2 = bf16[16,16,64,256]{3,2,1,0:T(8,128)(2,1)S(1)} collective-permute-done((bf16[16,16,64,256]{3,2,1,0:T(8,128)(2,1)}, bf16[16,16,64,256]{3,2,1,0:T(8,128)(2,1)S(1)}, u32[]{:S(2)}, u32[]{:S(2)}) %collective-permute-start.2) | collective-permute-done | bytes 8388640 | tf_op jit(solution)/shard_map/ppermute | solution.py:242
  224.9 187.7 %all_to_all.31 = bf16[16,16,64,256]{3,2,1,0:T(8,128)(2,1)} all-to-all(bf16[16,16,64,256]{3,2,1,0:T(8,128)(2,1)S(1)} %collective-permute-done.2), channel_id=1, replica_groups=mesh['pair'=2,'grp'=4,'sp'=4] {'grp','sp'}, dimensions={0} | all-to-all | bytes 16777216 | tf_op jit(solution)/shard_map/all_to_all | solution.py:246
  412.6 21.8 %collect.1 = (bf16[64,64,128]{2,1,0:T(8,128)(2,1)}, f32[384,128]{1,0:T(8,128)}) custom-call(s32[256]{0:T(256)} %reshape.98.wanted, bf16[256,64,256]{2,1,0:T(8,128)(2,1)} %bitcast.33, f32[64,64,256]{2,1,0:T(8,128)} %bitcast.38, bf16[64,64,128]{2,1,0:T(8,128)(2,1)} %bitcast.43, f32[64,64,128]{2,1,0:T(8,128)} %bitcast.42, bf16[64,64,128]{2,1,0:T(8,128)(2,1)} %bitcast.37, ...), custom_call_target="tpu_custom_call" | custom-call | tf_op jit(solution)/shard_map/collect/pallas_call | solution.py:361
  434.4 1.0 pad_maximum_fusion
  435.4 25.2 %all_to_all.32 = f32[32,48,128]{2,1,0:T(8,128)S(1)} all-to-all(f32[32,48,128]{2,1,0:T(8,128)S(1)} %bitcast.41), channel_id=1, replica_groups=mesh['pair'=2,'grp'=4,'sp'=4] {'pair','grp','sp'}, dimensions={0} | all-to-all | bytes 1572864 | tf_op jit(solution)/shard_map/all_to_all | solution.py:254
  460.7 24.2 %all_to_all.33 = f32[32,48,128]{2,1,0:T(8,128)S(1)} all-to-all(f32[32,48,128]{2,1,0:T(8,128)S(1)} %broadcast_in_dim.16), channel_id=1, replica_groups=mesh['pair'=2,'grp'=4,'sp'=4] {'pair','grp','sp'}, dimensions={0} | all-to-all | bytes 1572864 | tf_op jit(solution)/shard_map/all_to_all | solution.py:262
  485.0 0.6 slice.28
  485.6 0.7 fusion.4
  486.4 0.1 copy.33
  486.5 0.8 copy.35
  487.3 0.7 copy.38
  (11 shorter events, 0.5 us)
Async XLA Ops:
  4.9 1.3 collective-permute-start
  127.9 7.3 %collective-permute-start.1 = (bf16[16,16,64,128]{3,2,1,0:T(8,128)(2,1)S(1)}, bf16[16,16,64,128]{3,2,1,0:T(8,128)(2,1)}, u32[]{:S(2)}, u32[]{:S(2)}) collective-permute-start(bf16[16,16,64,128]{3,2,1,0:T(8,128)(2,1)S(1)} %all_to_all.30), channel_id=1, source_target_pairs={{0,16},{16,0},{1,17},{17,1},{2,18},{18,2},{3,19},{19,3},{4,20},{20... | collective-permute-start | bytes 12582920 | tf_op jit(solution)/shard_map/ppermute | solution.py:242
  211.4 13.4 %collective-permute-start.2 = (bf16[16,16,64,256]{3,2,1,0:T(8,128)(2,1)}, bf16[16,16,64,256]{3,2,1,0:T(8,128)(2,1)S(1)}, u32[]{:S(2)}, u32[]{:S(2)}) collective-permute-start(bf16[16,16,64,256]{3,2,1,0:T(8,128)(2,1)} %bitcast.50), channel_id=1, source_target_pairs={{0,16},{16,0},{1,17},{17,1},{2,18},{18,2},{3,19},{19,3},{4,20},{20... | collective-permute-start | bytes 25165832 | tf_op jit(solution)/shard_map/ppermute | solution.py:242
  412.6 21.8 %copy-start = (f32[1152,128]{1,0:T(8,128)S(1)}, f32[1152,128]{1,0:T(8,128)}, u32[]{:S(2)}) copy-start(f32[1152,128]{1,0:T(8,128)} %get-tuple-element.21) | copy-start | bytes 1769476

commit v2 on v1

v2 whole, which is shorter than its diff:
```python
import functools
import math

import jax
import jax.numpy as jnp
from jax import lax
from jax.experimental import pallas as pl
from jax.experimental.pallas import tpu as pltpu
from jax.sharding import PartitionSpec as P

HEADS = 4
GROUP_SIZE = 4
VMEM_LIMIT = 60 * 1024 * 1024


eps_norm = 1e-05
gelu_scale = 0.7978845608028654
gelu_cubic = 0.044715


def norm_rows(values):
    centred = values - jnp.mean(values, axis=-1, keepdims=True)
    factor = lax.rsqrt(jnp.mean(centred * centred, axis=-1, keepdims=True) + eps_norm)
    return (centred * factor, factor)


def norm_back(upstream, normed, factor):
    return factor * (
        upstream
        - jnp.mean(upstream, axis=-1, keepdims=True)
        - normed * jnp.mean(upstream * normed, axis=-1, keepdims=True)
    )


def gelu_pair(upper):
    squared = upper * upper
    tangent = jnp.tanh(gelu_scale * upper * (1.0 + gelu_cubic * squared))
    half = 0.5 * (1.0 + tangent)
    value = upper * half
    slope = half + 0.5 * upper * (1.0 - tangent * tangent) * (
        gelu_scale + (3.0 * gelu_cubic * gelu_scale) * squared
    )
    return (value, slope)


def matmul(former, latter):
    return jnp.dot(former, latter, preferred_element_type=jnp.float32)


def against(former, latter):
    return lax.dot_general(
        former, latter, (((1,), (1,)), ((), ())), preferred_element_type=jnp.float32
    )


def outer_sum(former, latter):
    return lax.dot_general(
        former, latter, (((0,), (0,)), ((), ())), preferred_element_type=jnp.float32
    )


def head_mask(window_len, width):
    row_head = lax.broadcasted_iota(jnp.int32, (HEADS * window_len, width), 0) // window_len
    col_head = lax.broadcasted_iota(jnp.int32, (HEADS * window_len, width), 1) // (width // HEADS)
    return jnp.where(row_head == col_head, 1.0, 0.0).astype(jnp.bfloat16)


def spread_heads(rows, mask):
    return jnp.concatenate([rows] * HEADS, axis=0) * mask


def gather_heads(full, window_len):
    width = full.shape[-1]
    lane = lax.broadcasted_iota(jnp.int32, (window_len, width), 1) // (width // HEADS)
    result = full[:window_len]
    for head in range(1, HEADS):
        result = jnp.where(lane == head, full[head * window_len : (head + 1) * window_len], result)
    return result


def pick_kernel(wanted, tokens, picked, normed):
    windows, window_len, width = tokens.shape

    @pl.loop(0, windows // 4)
    def _(step):
        rows = tokens[pl.ds(step * 4, 4)].astype(jnp.float32)
        normed[pl.ds(step * 4, 4)] = norm_rows(rows)[0].astype(jnp.bfloat16)

    @pl.loop(0, picked.shape[0] // 8)
    def _(step):
        for inner in range(8):
            slot = step * 8 + inner
            window = jnp.clip(wanted[slot], 0, windows - 1)
            picked[slot] = normed[window]


def first_kernel(
    position,
    tokens,
    cotangent,
    answered,
    weight_qkv,
    weight_out,
    weight_up,
    weight_down,
    resid_out,
    normed2_out,
    act_out,
    grad_upper_out,
    grad_resid_out,
    mixed_out,
    grad_mixed_out,
    query_out,
    kv_out,
    weights_out,
    self_values,
    outbound,
):
    step = pl.program_id(0)
    window_len = answered.shape[1]
    width = tokens.shape[-1]
    group = tokens.shape[0] // window_len
    fanout = kv_out.shape[1] // window_len - 1
    factor = 1.0 / math.sqrt(width // HEADS)
    mask = head_mask(window_len, width)

    rows = tokens[...].astype(jnp.float32)
    normed1_low = norm_rows(rows)[0].astype(jnp.bfloat16)
    qkv = matmul(normed1_low, weight_qkv[...]).astype(jnp.bfloat16)
    query_out[...] = qkv[:, :width]
    for item in range(group):
        own = slice(item * window_len, (item + 1) * window_len)
        far = jnp.concatenate(
            [answered[position[(step * group + item) * fanout + j]] for j in range(fanout)], axis=0
        )
        far_kv = matmul(far, weight_qkv[:, width:]).astype(jnp.bfloat16)
        kv = jnp.concatenate([qkv[own, width:], far_kv], axis=0)
        kv_out[item] = kv
        query = spread_heads(qkv[own, :width], mask)
        scores = against(kv[:, :width], query)
        peak = jnp.max(scores, axis=0, keepdims=True)
        powers = jnp.exp((scores - peak) * factor)
        weights = powers * (1.0 / jnp.sum(powers, axis=0, keepdims=True))
        weights_out[item] = weights
        full = outer_sum(weights.astype(jnp.bfloat16), kv[:, width:])
        mixed_out[own] = gather_heads(full, window_len).astype(jnp.bfloat16)

    mixed = mixed_out[...]
    cot = cotangent[...]
    resid_low = (rows + matmul(mixed, weight_out[...])).astype(jnp.bfloat16)
    resid_out[...] = resid_low
    normed2, factor2 = norm_rows(resid_low.astype(jnp.float32))
    normed2_low = normed2.astype(jnp.bfloat16)
    normed2_out[...] = normed2_low
    value, slope = gelu_pair(matmul(normed2_low, weight_up[...]))
    act_out[...] = value.astype(jnp.bfloat16)
    grad_upper = (against(cot, weight_down[...]) * slope).astype(jnp.bfloat16)
    grad_upper_out[...] = grad_upper
    grad_resid = cot.astype(jnp.float32) + norm_back(
        against(grad_upper, weight_up[...]), normed2, factor2
    )
    grad_resid_out[...] = grad_resid
    grad_mixed = against(grad_resid.astype(jnp.bfloat16), weight_out[...]).astype(jnp.bfloat16)
    grad_mixed_out[...] = grad_mixed

    for item in range(group):
        own = slice(item * window_len, (item + 1) * window_len)
        head_grad = spread_heads(grad_mixed[own], mask)
        grad_values = matmul(weights_out[item].astype(jnp.bfloat16), head_grad)
        self_values[own] = grad_values[:window_len]
        for j in range(fanout):
            slot = position[(step * group + item) * fanout + j]
            source = slice((j + 1) * window_len, (j + 2) * window_len)
            outbound[slot] = grad_values[source].astype(jnp.bfloat16)


def second_kernel(
    position,
    tokens,
    cotangent,
    resid,
    normed2_low,
    act,
    grad_upper,
    grad_resid,
    mixed,
    grad_mixed,
    query_rows,
    kv_rows,
    weights_rows,
    weight_down,
    block_out,
    grad_query_out,
    self_keys,
    outbound,
    weight_grads,
):
    step = pl.program_id(0)
    window_len = outbound.shape[1]
    width = cotangent.shape[-1]
    group = cotangent.shape[0] // window_len
    fanout = kv_rows.shape[1] // window_len - 1
    factor = 1.0 / math.sqrt(width // HEADS)
    mask = head_mask(window_len, width)

    @pl.when(step == 0)
    def _():
        weight_grads[...] = jnp.zeros_like(weight_grads)

    for item in range(group):
        own = slice(item * window_len, (item + 1) * window_len)
        kv = kv_rows[item]
        weights = weights_rows[item]
        query = spread_heads(query_rows[own], mask)
        head_grad = spread_heads(grad_mixed[own], mask)
        grad_weights = against(kv[:, width:], head_grad)
        inner = jnp.sum(grad_weights * weights, axis=0, keepdims=True)
        grad_scores = (weights * (grad_weights - inner) * factor).astype(jnp.bfloat16)
        full = outer_sum(grad_scores, kv[:, :width])
        grad_query_out[own] = gather_heads(full, window_len).astype(jnp.bfloat16)
        grad_keys = matmul(grad_scores, query)
        self_keys[own] = grad_keys[:window_len]
        for j in range(fanout):
            slot = position[(step * group + item) * fanout + j]
            source = slice((j + 1) * window_len, (j + 2) * window_len)
            outbound[slot] = grad_keys[source].astype(jnp.bfloat16)

    cot = cotangent[...]
    block_out[...] = (
        resid[...].astype(jnp.float32) + matmul(act[...], weight_down[...])
    ).astype(jnp.bfloat16)
    grad_up = outer_sum(normed2_low[...], grad_upper[...])
    blocks = grad_upper.shape[-1] // width
    normed1_low = norm_rows(tokens[...].astype(jnp.float32))[0].astype(jnp.bfloat16)
    weight_grads[:width] += outer_sum(normed1_low, grad_query_out[...])
    weight_grads[width : 2 * width] += outer_sum(mixed[...], grad_resid[...].astype(jnp.bfloat16))
    for block in range(blocks):
        weight_grads[(2 + block) * width : (3 + block) * width] += grad_up[
            :, block * width : (block + 1) * width
        ]
    weight_grads[(2 + blocks) * width :] += outer_sum(act[...], cot)


def add_returned(wanted, returned, own, total):
    step = pl.program_id(0)
    windows = total.shape[0]
    slots = returned.shape[0]

    @pl.when(step == 0)
    def _():
        total[...] = own[...]

    for slot in range(slots):
        window = wanted[step * slots + slot]

        @pl.when(window < windows)
        def _():
            total[window] += returned[slot].astype(jnp.float32)


def value_kernel(
    wanted, returned, self_values, grad_query, tokens, weight_qkv, upstream, weight_grads, total
):
    windows, window_len, width = tokens.shape
    count = GROUP_SIZE * window_len
    add_returned(wanted, returned, self_values, total)

    @pl.when(pl.program_id(0) == pl.num_programs(0) - 1)
    def _():
        weight_grads[...] = jnp.zeros_like(weight_grads)

        @pl.loop(0, windows // GROUP_SIZE)
        def _(part):
            span = pl.ds(part * GROUP_SIZE, GROUP_SIZE)
            normed1, _ = norm_rows(tokens[span].reshape(count, width).astype(jnp.float32))
            grads = total[span].reshape(count, width).astype(jnp.bfloat16)
            queries = grad_query[span].reshape(count, width)
            partial = against(queries, weight_qkv[:, :width]) + against(
                grads, weight_qkv[:, 2 * width :]
            )
            upstream[span] = partial.reshape(GROUP_SIZE, window_len, width)
            weight_grads[...] += outer_sum(normed1.astype(jnp.bfloat16), grads)


def key_kernel(
    wanted,
    returned,
    self_keys,
    upstream,
    grad_resid,
    tokens,
    weight_qkv,
    grad_tokens,
    weight_grads,
    total,
):
    windows, window_len, width = tokens.shape
    count = GROUP_SIZE * window_len
    add_returned(wanted, returned, self_keys, total)

    @pl.when(pl.program_id(0) == pl.num_programs(0) - 1)
    def _():
        weight_grads[...] = jnp.zeros_like(weight_grads)

        @pl.loop(0, windows // GROUP_SIZE)
        def _(part):
            span = pl.ds(part * GROUP_SIZE, GROUP_SIZE)
            normed1, factor1 = norm_rows(tokens[span].reshape(count, width).astype(jnp.float32))
            grads = total[span].reshape(count, width).astype(jnp.bfloat16)
            towards = upstream[span].reshape(count, width) + against(
                grads, weight_qkv[:, width : 2 * width]
            )
            result = grad_resid[span].reshape(count, width) + norm_back(towards, normed1, factor1)
            grad_tokens[span] = result.astype(jnp.bfloat16).reshape(GROUP_SIZE, window_len, width)
            weight_grads[...] += outer_sum(normed1.astype(jnp.bfloat16), grads)


def swapped(value):
    return lax.ppermute(value, "pair", [(0, 1), (1, 0)])


def deliver(parcel):
    return lax.all_to_all(parcel, ("grp", "sp"), split_axis=0, concat_axis=0, tiled=True)


ALL = ("pair", "grp", "sp")


def summed(rows):
    devices = lax.axis_size(ALL)
    share = lax.all_to_all(
        rows.reshape(devices, rows.shape[0] // devices, rows.shape[1]),
        ALL,
        split_axis=0,
        concat_axis=0,
        tiled=True,
    )
    copies = jnp.broadcast_to(jnp.sum(share, axis=0)[None], share.shape)
    copies = lax.all_to_all(copies, ALL, split_axis=0, concat_axis=0, tiled=True)
    return copies.reshape(rows.shape)


def whole(shape):
    return pl.BlockSpec(shape, lambda *_: (0,) * len(shape))


def body(tokens, owner_ids, local_ids, weight_qkv, weight_out, weight_up, weight_down, cotangent):
    holders = lax.axis_size("grp") * lax.axis_size("sp")
    width = tokens.shape[-1]
    hidden = weight_up.shape[-1]
    windows = tokens.shape[1]
    window_len = tokens.shape[2]
    fanout = owner_ids.shape[-1]
    slots = max(2, 2 * windows * fanout // holders)
    keys_len = (fanout + 1) * window_len
    rows_total = windows * window_len
    group = GROUP_SIZE
    group_rows = group * window_len
    token_rows = tokens[0].reshape(rows_total, width)
    cot_rows = cotangent[0].reshape(rows_total, width)
    params = pltpu.CompilerParams(vmem_limit_bytes=VMEM_LIMIT)

    owners = owner_ids[0].reshape(-1)
    local_rows = local_ids[0].reshape(-1)
    onehot = (owners[:, None] == jnp.arange(holders, dtype=jnp.int32)[None, :]).astype(jnp.int32)
    ranks = jnp.sum((jnp.cumsum(onehot, axis=0) - 1) * onehot, axis=1)
    position = owners * slots + ranks
    requests = (
        jnp.full((holders * slots,), windows, jnp.int32)
        .at[position]
        .set(local_rows)
        .reshape(holders, slots)
    )
    wanted_flat = deliver(swapped(requests)).reshape(-1)

    picked = pl.pallas_call(
        pick_kernel,
        grid_spec=pltpu.PrefetchScalarGridSpec(
            num_scalar_prefetch=1,
            grid=(1,),
            in_specs=[whole((windows, window_len, width))],
            out_specs=whole((holders * slots, window_len, width)),
            scratch_shapes=[pltpu.VMEM((windows, window_len, width), jnp.bfloat16)],
        ),
        out_shape=jax.ShapeDtypeStruct((holders * slots, window_len, width), jnp.bfloat16),
        compiler_params=params,
        name="pick",
    )(wanted_flat, tokens[0])
    answered = swapped(deliver(picked.reshape(holders, slots, window_len, width)))
    answered = answered.reshape(holders * slots, window_len, width)

    blocks = hidden // width
    span_heads = HEADS * window_len
    slot_shape = (holders * slots, window_len, width)
    window_shape = (windows, window_len, width)
    grad_rows_shape = ((2 + 2 * blocks) * width, width)

    def row_spec(lanes):
        return pl.BlockSpec((group_rows, lanes), lambda i, *_: (i, 0))

    def window_spec(lanes):
        return pl.BlockSpec((group, keys_len, lanes), lambda i, *_: (i, 0, 0))

    def row_shape(lanes, kind=jnp.bfloat16):
        return jax.ShapeDtypeStruct((rows_total, lanes), kind)

    saved_specs = [
        row_spec(width),
        row_spec(width),
        row_spec(hidden),
        row_spec(hidden),
        row_spec(width),
        row_spec(width),
        row_spec(width),
        row_spec(width),
        window_spec(2 * width),
        window_spec(span_heads),
    ]
    *saved, self_values, outbound_values = pl.pallas_call(
        first_kernel,
        grid_spec=pltpu.PrefetchScalarGridSpec(
            num_scalar_prefetch=1,
            grid=(windows // group,),
            in_specs=[
                row_spec(width),
                row_spec(width),
                whole(slot_shape),
                whole((width, 3 * width)),
                whole((width, width)),
                whole((width, hidden)),
                whole((hidden, width)),
            ],
            out_specs=saved_specs + [row_spec(width), whole(slot_shape)],
        ),
        out_shape=[
            row_shape(width),
            row_shape(width),
            row_shape(hidden),
            row_shape(hidden),
            row_shape(width, jnp.float32),
            row_shape(width),
            row_shape(width),
            row_shape(width),
            jax.ShapeDtypeStruct((windows, keys_len, 2 * width), jnp.bfloat16),
            jax.ShapeDtypeStruct((windows, keys_len, span_heads), jnp.float32),
            row_shape(width, jnp.float32),
            jax.ShapeDtypeStruct(slot_shape, jnp.bfloat16),
        ],
        compiler_params=params,
        name="attend_and_tail",
    )(position, token_rows, cot_rows, answered, weight_qkv, weight_out, weight_up, weight_down)
    grad_resid = saved[4]

    def across(outbound):
        return swapped(outbound.reshape(holders, slots, window_len, width))

    outgoing_values, saved = lax.optimization_barrier((across(outbound_values), saved))
    returned_values = deliver(outgoing_values).reshape(slot_shape)

    out_rows, grad_query, self_keys, outbound_keys, tail_grads = pl.pallas_call(
        second_kernel,
        grid_spec=pltpu.PrefetchScalarGridSpec(
            num_scalar_prefetch=1,
            grid=(windows // group,),
            in_specs=[row_spec(width), row_spec(width)] + saved_specs + [whole((hidden, width))],
            out_specs=[
                row_spec(width),
                row_spec(width),
                row_spec(width),
                whole(slot_shape),
                whole(grad_rows_shape),
            ],
        ),
        out_shape=[
            row_shape(width),
            row_shape(width),
            row_shape(width, jnp.float32),
            jax.ShapeDtypeStruct(slot_shape, jnp.bfloat16),
            jax.ShapeDtypeStruct(grad_rows_shape, jnp.float32),
        ],
        compiler_params=params,
        cost_estimate=pl.CostEstimate(
            flops=40 * 10**9, bytes_accessed=150 * 10**6, transcendentals=0
        ),
        name="key_gradients",
    )(position, token_rows, cot_rows, *saved, weight_down)

    outgoing_keys, returned_values, grad_query = lax.optimization_barrier(
        (across(outbound_keys), returned_values, grad_query)
    )
    returned_keys = deliver(outgoing_keys).reshape(slot_shape)

    slot_spec = pl.BlockSpec((slots, window_len, width), lambda i, *_: (i, 0, 0))
    collect_scratch = [pltpu.VMEM(window_shape, jnp.float32)]
    upstream, value_grads = pl.pallas_call(
        value_kernel,
        grid_spec=pltpu.PrefetchScalarGridSpec(
            num_scalar_prefetch=1,
            grid=(holders,),
            in_specs=[slot_spec] + [whole(window_shape)] * 3 + [whole((width, 3 * width))],
            out_specs=[whole(window_shape), whole((width, width))],
            scratch_shapes=collect_scratch,
        ),
        out_shape=[
            jax.ShapeDtypeStruct(window_shape, jnp.float32),
            jax.ShapeDtypeStruct((width, width), jnp.float32),
        ],
        compiler_params=params,
        cost_estimate=pl.CostEstimate(
            flops=10 * 10**9, bytes_accessed=50 * 10**6, transcendentals=0
        ),
        name="collect_values",
    )(
        wanted_flat,
        returned_values,
        self_values.reshape(window_shape),
        grad_query.reshape(window_shape),
        tokens[0],
        weight_qkv,
    )
    inv_count = 1.0 / math.sqrt(2 * windows * holders * window_len)
    tail_sums = (lax.psum(tail_grads, ALL) * inv_count).reshape(2 + 2 * blocks, width, width)

    grad_rows, key_grads = pl.pallas_call(
        key_kernel,
        grid_spec=pltpu.PrefetchScalarGridSpec(
            num_scalar_prefetch=1,
            grid=(holders,),
            in_specs=[slot_spec] + [whole(window_shape)] * 4 + [whole((width, 3 * width))],
            out_specs=[whole(window_shape), whole((width, width))],
            scratch_shapes=collect_scratch,
        ),
        out_shape=[
            jax.ShapeDtypeStruct(window_shape, jnp.bfloat16),
            jax.ShapeDtypeStruct((width, width), jnp.float32),
        ],
        compiler_params=params,
        name="collect_keys",
    )(
        wanted_flat,
        returned_keys,
        self_keys.reshape(window_shape),
        upstream,
        grad_resid.reshape(window_shape),
        tokens[0],
        weight_qkv,
    )
    kv_sums = summed(jnp.concatenate([key_grads, value_grads], axis=0)) * inv_count

    return (
        out_rows.reshape(1, windows, window_len, width),
        grad_rows[None],
        jnp.concatenate([tail_sums[0], kv_sums[:width], kv_sums[width:]], axis=1),
        tail_sums[1],
        tail_sums[2 : 2 + blocks].transpose(1, 0, 2).reshape(width, hidden),
        tail_sums[2 + blocks :].reshape(hidden, width),
    )


def solution(mesh):
    in_specs = (
        P("pair", ("grp", "sp"), None, None),
        P("pair", ("grp", "sp"), None),
        P("pair", ("grp", "sp"), None),
        P(),
        P(),
        P(),
        P(),
        P("pair", ("grp", "sp"), None, None),
    )
    out_specs = (
        P("pair", ("grp", "sp"), None, None),
        P("pair", ("grp", "sp"), None, None),
        P(),
        P(),
        P(),
        P(),
    )
    return jax.shard_map(body, mesh=mesh, in_specs=in_specs, out_specs=out_specs, check_vma=False)
```

time: 489 us -> 517 us (1.057)
  blocking collectives: 349 us -> 112 us
  waiting for transfers between devices: 20.8 us -> 190 us
  starting transfers between devices: 0.67 us -> 49 us
  Pallas kernels: 106 us -> 136 us
  between operations: 0.71 us -> 14.2 us
    all_to_all x3 -> x2, blocking collectives: 300 us -> 112 us  [deliver(): lax.all_to_all(parcel, ('grp', 'sp'), split_axis=0, concat_axis=0, tiled=...]
    all_to_all x0 -> x4, waiting for transfers between devices: none -> 109 us  [the longest x2 103 us: deliver(): lax.all_to_all(parcel, ('grp', 'sp'), split_axis=0, concat_axis=0, tiled=...]
    psum x0 -> x1, waiting for transfers between devices: none -> 57.9 us  [body(): lax.psum(tail_grads, ALL) * inv_count]
    all_to_all x2 -> x0, blocking collectives: 49.4 us -> none  [the longest x1 25.2 us: summed(): lax.all_to_all(rows.reshape(devices, rows.shape[0] // devices, rows.shape...]
    all_to_all x0 -> x4, starting transfers between devices: none -> 48.1 us  [the longest x2 25.1 us: deliver(): lax.all_to_all(parcel, ('grp', 'sp'), split_axis=0, concat_axis=0, tiled=...]
    pallas_call x2 -> x4, Pallas kernels: 98 us -> 128 us  [the longest x1 57.2 us: body(): pl.pallas_call(first_kernel, grid_spec=pltpu.PrefetchScalarGridSpec(num_s...]
    ppermute x3 -> x4, waiting for transfers between devices: 20.8 us -> 22.2 us  [swapped(): return lax.ppermute(value, 'pair', [(0, 1), (1, 0)])]
  transfers between devices with their start and end apart: 3 -> 9, of which waited for: 3 -> 8; matrix products, arithmetic and copies ran while one was open for 0% -> 1% of each run, Pallas kernels for 0% -> 14%
where the time goes in v2:
time: 517 us; the launch traced here: 516 us
  waiting for transfers between devices  190 us (37%)
  Pallas kernels  136 us (26%)
  blocking collectives  112 us (22%)
  starting transfers between devices  49 us (9%)
  between operations  14.2 us (3%)
  local copies, waits for them, and re-layouts  9.02 us (2%)
  other arithmetic  5.7 us (1%)
    all_to_all x2, blocking collectives, deliver(): lax.all_to_all(parcel, ('grp', 'sp'), split_axis=0, concat_axis=0, tiled=...  112 us
    all_to_all x2, waiting for transfers between devices, deliver(): lax.all_to_all(parcel, ('grp', 'sp'), split_axis=0, concat_axis=0, tiled=...  103 us
    psum x1, waiting for transfers between devices, body(): lax.psum(tail_grads, ALL) * inv_count  57.9 us
    pallas_call x1, Pallas kernels, body(): pl.pallas_call(first_kernel, grid_spec=pltpu.PrefetchScalarGridSpec(num_s...  57.2 us
    pallas_call x1, Pallas kernels, body(): pl.pallas_call(second_kernel, grid_spec=pltpu.PrefetchScalarGridSpec(num_...  32.1 us
    all_to_all x2, starting transfers between devices, deliver(): lax.all_to_all(parcel, ('grp', 'sp'), split_axis=0, concat_axis=0, tiled=...  25.1 us
    ppermute x4, waiting for transfers between devices, swapped(): return lax.ppermute(value, 'pair', [(0, 1), (1, 0)])  22.2 us
    pallas_call x1, Pallas kernels, body(): pl.pallas_call(key_kernel, grid_spec=pltpu.PrefetchScalarGridSpec(num_sca...  19.8 us
  transfers between devices with their start and end apart: 9, of which 8 were waited for; matrix products, arithmetic and copies ran while one was open for 1% of the time, Pallas kernels for 14%

profile of v2, /device:TPU:0, one launch (start us, length us, event | category | flops | bytes accessed | tf_op | source)
XLA Modules:
  0.0 515.6 jit_solution(10274557478626466587)
XLA Ops:
  7.2 0.7 broadcast_multiply_fusion.2
  7.8 0.8 copy.22
  8.9 0.8 copy.24
  10.4 1.0 scatter_custom_fusion
  11.9 0.8 collective-permute-done
  12.7 15.3 %all_to_all.34 = s32[16,1,16]{2,1,0:T(1,128)S(1)} all-to-all(s32[16,1,16]{2,1,0:T(1,128)S(1)} %bitcast.48), channel_id=1, replica_groups=mesh['pair'=2,'grp'=4,'sp'=4] {'grp','sp'}, dimensions={0} | all-to-all | bytes 2048 | tf_op jit(solution)/shard_map/all_to_all | solution.py:323
  28.5 0.7 reduce.3
  29.8 7.8 %pick.1 = bf16[256,64,128]{2,1,0:T(8,128)(2,1)} custom-call(s32[256]{0:T(256)} %reshape.105.wanted, bf16[64,64,128]{2,1,0:T(8,128)(2,1)} %bitcast.37), custom_call_target="tpu_custom_call" | custom-call | tf_op jit(solution)/shard_map/pick/pallas_call | solution.py:376
  37.6 96.9 %all_to_all.35 = bf16[16,16,64,128]{3,2,1,0:T(8,128)(2,1)S(1)} all-to-all(bf16[16,16,64,128]{3,2,1,0:T(8,128)(2,1)} %bitcast.36), channel_id=1, replica_groups=mesh['pair'=2,'grp'=4,'sp'=4] {'grp','sp'}, dimensions={0} | all-to-all | bytes 8388608 | tf_op jit(solution)/shard_map/all_to_all | solution.py:323
  135.0 6.8 %collective-permute-done.1 = bf16[16,16,64,128]{3,2,1,0:T(8,128)(2,1)} collective-permute-done((bf16[16,16,64,128]{3,2,1,0:T(8,128)(2,1)S(1)}, bf16[16,16,64,128]{3,2,1,0:T(8,128)(2,1)}, u32[]{:S(2)}, u32[]{:S(2)}) %collective-permute-start.1) | collective-permute-done | bytes 4194336 | tf_op jit(solution)/shard_map/ppermute | solution.py:319
  141.8 57.2 %attend_and_tail.1 = (bf16[4096,128]{1,0:T(8,128)(2,1)}, bf16[4096,128]{1,0:T(8,128)(2,1)}, bf16[4096,512]{1,0:T(8,128)(2,1)}, bf16[4096,512]{1,0:T(8,128)(2,1)}...) custom-call(s32[128]{0:T(128)} %multiply_add_fusion.position, ...), custom_call_target="tpu_custom_call" | custom-call | tf_op jit(solution)/shard_map/attend_and_tail/pallas_call | solution.py:419
  199.2 7.2 %collective-permute-done.2 = bf16[16,16,64,128]{3,2,1,0:T(8,128)(2,1)S(1)} collective-permute-done((bf16[16,16,64,128]{3,2,1,0:T(8,128)(2,1)}, bf16[16,16,64,128]{3,2,1,0:T(8,128)(2,1)S(1)}, u32[]{:S(2)}, u32[]{:S(2)}) %collective-permute-start.2) | collective-permute-done | bytes 4194336 | tf_op jit(solution)/shard_map/ppermute | solution.py:319
  206.5 2.0 copy-done
  208.4 4.5 all-to-all-start.2
  213.0 32.1 %key_gradients.1 = (bf16[4096,128]{1,0:T(8,128)(2,1)}, bf16[4096,128]{1,0:T(8,128)(2,1)}, f32[4096,128]{1,0:T(8,128)}, bf16[256,64,128]{2,1,0:T(8,128)(2,1)}, f32[1280,128]{1,0:T(8,128)}) custom-call(s32[128]{0:T(128)} %multiply_add_fusion.position, bf16[4096,128]{1,0:T(8,128)(2,1)} %bitcast.39, bf16[4096,128]{1,0:T(8,128)(2,1)} %bitcast.46, ...), custom_call_target="tpu_custom_call" | custom-call | flops 40000000000 | bytes 150000000 | tf_op jit(solution)/shard_map/key_gradients/pallas_call | solution.py:460
  245.3 7.4 %collective-permute-done.3 = bf16[16,16,64,128]{3,2,1,0:T(8,128)(2,1)} collective-permute-done((bf16[16,16,64,128]{3,2,1,0:T(8,128)(2,1)}, bf16[16,16,64,128]{3,2,1,0:T(8,128)(2,1)}, u32[]{:S(2)}, u32[]{:S(2)}) %collective-permute-start.3) | collective-permute-done | bytes 4194336 | tf_op jit(solution)/shard_map/ppermute | solution.py:319
  252.6 41.2 %all-to-all-done.2 = bf16[16,16,64,128]{3,2,1,0:T(8,128)(2,1)} async-done(((bf16[16,16,64,128]{3,2,1,0:T(8,128)(2,1)}), bf16[16,16,64,128]{3,2,1,0:T(8,128)(2,1)}, u32[]{:S(2)}, u32[]{:S(2)}) %all-to-all-start.2) | async-done | bytes 4194336 | tf_op jit(solution)/shard_map/all_to_all | solution.py:323
  293.8 20.6 %all-to-all-start.3 = ((bf16[16,16,64,128]{3,2,1,0:T(8,128)(2,1)}), bf16[16,16,64,128]{3,2,1,0:T(8,128)(2,1)}, u32[]{:S(2)}, u32[]{:S(2)}) async-start(bf16[16,16,64,128]{3,2,1,0:T(8,128)(2,1)} %collective-permute-done.3), calls=%async_computation.3 | async-start | bytes 8388608 | tf_op jit(solution)/shard_map/all_to_all | solution.py:323
  314.4 0.7 all-reduce.2.cloned.1.call-update
  315.1 19.0 %collect_values.1 = (f32[64,64,128]{2,1,0:T(8,128)}, f32[128,128]{1,0:T(8,128)}) custom-call(s32[256]{0:T(256)} %reshape.105.wanted, bf16[256,64,128]{2,1,0:T(8,128)(2,1)} %bitcast.11.returned, f32[64,64,128]{2,1,0:T(8,128)} %bitcast.51, bf16[64,64,128]{2,1,0:T(8,128)(2,1)} %bitcast.54, bf16[64,64,128]{2,1,0:T(8,128)(2,1)} %bitcast.40, ...), custom_call_target="tpu_custom_call" | custom-call | flops 10000000000 | bytes 50000000 | tf_op jit(solution)/shard_map/collect_values/pallas_call | solution.py:495
  334.1 62.0 %all-to-all-done.3 = bf16[16,16,64,128]{3,2,1,0:T(8,128)(2,1)} async-done(((bf16[16,16,64,128]{3,2,1,0:T(8,128)(2,1)}), bf16[16,16,64,128]{3,2,1,0:T(8,128)(2,1)}, u32[]{:S(2)}, u32[]{:S(2)}) %all-to-all-start.3) | async-done | bytes 4194336 | tf_op jit(solution)/shard_map/all_to_all | solution.py:323
  396.1 19.8 %collect_keys.1 = (bf16[64,64,128]{2,1,0:T(8,128)(2,1)}, f32[128,128]{1,0:T(8,128)}) custom-call(s32[256]{0:T(256)} %reshape.105.wanted, bf16[256,64,128]{2,1,0:T(8,128)(2,1)} %bitcast.12.returned, f32[64,64,128]{2,1,0:T(8,128)} %bitcast.43, f32[64,64,128]{2,1,0:T(8,128)} %get-tuple-element.71.upstream, f32[64,64,128]{2,1,0:T(8,128)} %bitcast.42, ...), custom_call_target="tpu_custom_call" | custom-call | tf_op jit(solution)/shard_map/collect_keys/pallas_call | solution.py:524
  415.9 1.5 maximum_bitcast_fusion
  417.4 19.4 %all-to-all-start.4 = ((f32[32,8,128]{2,1,0:T(8,128)}), f32[32,8,128]{2,1,0:T(8,128)S(1)}, u32[]{:S(2)}, u32[]{:S(2)}) async-start(f32[32,8,128]{2,1,0:T(8,128)} %maximum_bitcast_fusion), calls=%async_computation.4 | async-start | bytes 262144 | tf_op jit(solution)/shard_map/all_to_all | solution.py:331
  436.8 57.9 %all-reduce.2.cloned.1.call-done = f32[1280,128]{1,0:T(8,128)} async-done(((f32[1280,128]{1,0:T(8,128)}), f32[1280,128]{1,0:T(8,128)}) %all-reduce.2.cloned.1.call-update) | async-done | bytes 655376 | tf_op jit(solution)/shard_map/psum | solution.py:522
  494.6 1.1 broadcast_multiply_fusion
  495.8 0.7 broadcast_in_dim.16
  496.5 3.6 all-to-all-start.5
  500.1 0.7 fusion.4
  500.9 0.7 copy.28
  502.2 5.8 %all-to-all-done.5 = f32[32,8,128]{2,1,0:T(8,128)S(1)} async-done(((f32[32,8,128]{2,1,0:T(8,128)}), f32[32,8,128]{2,1,0:T(8,128)S(1)}, u32[]{:S(2)}, u32[]{:S(2)}) %all-to-all-start.5) | async-done | bytes 131104 | tf_op jit(solution)/shard_map/all_to_all | solution.py:339
  508.1 0.7 pad_maximum_fusion
  (25 shorter events, 4.3 us)
Async XLA Ops:
  11.4 1.3 collective-permute-start
  134.5 7.3 %collective-permute-start.1 = (bf16[16,16,64,128]{3,2,1,0:T(8,128)(2,1)S(1)}, bf16[16,16,64,128]{3,2,1,0:T(8,128)(2,1)}, u32[]{:S(2)}, u32[]{:S(2)}) collective-permute-start(bf16[16,16,64,128]{3,2,1,0:T(8,128)(2,1)S(1)} %all_to_all.35), channel_id=1, source_target_pairs={{0,16},{16,0},{1,17},{17,1},{2,18},{18,2},{3,19},{19,3},{4,20},{20... | collective-permute-start | bytes 12582920 | tf_op jit(solution)/shard_map/ppermute | solution.py:319
  199.0 7.4 %collective-permute-start.2 = (bf16[16,16,64,128]{3,2,1,0:T(8,128)(2,1)}, bf16[16,16,64,128]{3,2,1,0:T(8,128)(2,1)S(1)}, u32[]{:S(2)}, u32[]{:S(2)}) collective-permute-start(bf16[16,16,64,128]{3,2,1,0:T(8,128)(2,1)} %bitcast.50), channel_id=1, source_target_pairs={{0,16},{16,0},{1,17},{17,1},{2,18},{18,2},{3,19},{19,3},{4,20},{20... | collective-permute-start | bytes 12582920 | tf_op jit(solution)/shard_map/ppermute | solution.py:319
  206.5 2.0 copy-start
  208.4 85.4 %all-to-all-start.2 = ((bf16[16,16,64,128]{3,2,1,0:T(8,128)(2,1)}), bf16[16,16,64,128]{3,2,1,0:T(8,128)(2,1)}, u32[]{:S(2)}, u32[]{:S(2)}) async-start(bf16[16,16,64,128]{3,2,1,0:T(8,128)(2,1)} %copy-done), calls=%async_computation.2 | async-start | bytes 8388608 | tf_op jit(solution)/shard_map/all_to_all | solution.py:323
  245.1 7.6 %collective-permute-start.3 = (bf16[16,16,64,128]{3,2,1,0:T(8,128)(2,1)}, bf16[16,16,64,128]{3,2,1,0:T(8,128)(2,1)}, u32[]{:S(2)}, u32[]{:S(2)}) collective-permute-start(bf16[16,16,64,128]{3,2,1,0:T(8,128)(2,1)} %bitcast.49), channel_id=1, source_target_pairs={{0,16},{16,0},{1,17},{17,1},{2,18},{18,2},{3,19},{19,3},{4,20},{20... | collective-permute-start | bytes 12582920 | tf_op jit(solution)/shard_map/ppermute | solution.py:319
  293.8 102.3 %all-to-all-start.3 = ((bf16[16,16,64,128]{3,2,1,0:T(8,128)(2,1)}), bf16[16,16,64,128]{3,2,1,0:T(8,128)(2,1)}, u32[]{:S(2)}, u32[]{:S(2)}) async-start(bf16[16,16,64,128]{3,2,1,0:T(8,128)(2,1)} %collective-permute-done.3), calls=%async_computation.3 | async-start | bytes 8388608 | tf_op jit(solution)/shard_map/all_to_all | solution.py:323
  314.4 180.3 %all-reduce.2.cloned.1.call-start = ((), (), s32[]{:S(2)}) async-start(), calls=%async_computation.6 | async-start | bytes 1310720 | tf_op jit(solution)/shard_map/psum | solution.py:522
  396.1 19.8 %copy-start.1 = (f32[128,128]{1,0:T(8,128)S(1)}, f32[128,128]{1,0:T(8,128)}, u32[]{:S(2)}) copy-start(f32[128,128]{1,0:T(8,128)} %get-tuple-element.75) | copy-start | bytes 196612
  417.4 78.4 %all-to-all-start.4 = ((f32[32,8,128]{2,1,0:T(8,128)}), f32[32,8,128]{2,1,0:T(8,128)S(1)}, u32[]{:S(2)}, u32[]{:S(2)}) async-start(f32[32,8,128]{2,1,0:T(8,128)} %maximum_bitcast_fusion), calls=%async_computation.4 | async-start | bytes 262144 | tf_op jit(solution)/shard_map/all_to_all | solution.py:331
  496.5 11.5 %all-to-all-start.5 = ((f32[32,8,128]{2,1,0:T(8,128)}), f32[32,8,128]{2,1,0:T(8,128)S(1)}, u32[]{:S(2)}, u32[]{:S(2)}) async-start(f32[32,8,128]{2,1,0:T(8,128)} %broadcast_in_dim.16), calls=%async_computation.5 | async-start | bytes 262144 | tf_op jit(solution)/shard_map/all_to_all | solution.py:339
Sparse Core Ops, SparseCore 0:
  320.4 174.1 all-reduce.1

commit v3 on v2

--- a/solution.py
+++ b/solution.py
@@ -326,18 +326,101 @@
 ALL = ("pair", "grp", "sp")
 
 
-def summed(rows):
-    devices = lax.axis_size(ALL)
-    share = lax.all_to_all(
-        rows.reshape(devices, rows.shape[0] // devices, rows.shape[1]),
-        ALL,
-        split_axis=0,
-        concat_axis=0,
-        tiled=True,
-    )
-    copies = jnp.broadcast_to(jnp.sum(share, axis=0)[None], share.shape)
-    copies = lax.all_to_all(copies, ALL, split_axis=0, concat_axis=0, tiled=True)
-    return copies.reshape(rows.shape)
+def sum_kernel(scatter, scale, rows, total, pair_part, pair_sum, sp_part, sp_sum, grp_part, mine, sp_full, half, pair_full, send_sems, recv_sems):
+    sizes = {axis: lax.axis_size(axis) for axis in ALL}
+    place = {axis: lax.axis_index(axis) for axis in ALL}
+    used = [0]
+
+    barrier = pltpu.get_barrier_semaphore()
+    for axis in ALL:
+        for hop in range(1, sizes[axis]):
+            pl.semaphore_signal(
+                barrier,
+                inc=1,
+                device_id={axis: lax.rem(place[axis] + hop, sizes[axis])},
+                device_id_type=pl.DeviceIdType.MESH,
+            )
+    pl.semaphore_wait(barrier, sum(sizes[axis] - 1 for axis in ALL))
+
+    def exchange(axis, source, landing):
+        copies = []
+        for hop in range(1, sizes[axis]):
+            target = lax.rem(place[axis] + hop, sizes[axis])
+            copy = pltpu.make_async_remote_copy(
+                src_ref=source(target),
+                dst_ref=landing.at[place[axis]],
+                send_sem=send_sems.at[used[0]],
+                recv_sem=recv_sems.at[used[0]],
+                device_id={axis: target},
+                device_id_type=pl.DeviceIdType.MESH,
+            )
+            copy.start()
+            used[0] += 1
+            copies.append(copy)
+        landing[place[axis]] = source(place[axis])[...]
+        for copy in copies:
+            copy.wait()
+
+    def added(landing):
+        result = landing[0]
+        for index in range(1, landing.shape[0]):
+            result = result + landing[index]
+        return result
+
+    exchange("pair", lambda target: rows.at[target], pair_part)
+    pieces, count, _ = pair_sum.shape
+    for piece in range(pieces):
+        span = slice(piece * count, (piece + 1) * count)
+        pair_sum[piece] = pair_part[0, span] + pair_part[1, span]
+    exchange("sp", (lambda target: pair_sum.at[target]) if scatter else (lambda _: pair_sum.at[0]), sp_part)
+    sp_sum[...] = added(sp_part)
+    exchange("grp", lambda _: sp_sum, grp_part)
+    mine[...] = added(grp_part) * scale
+    if scatter:
+        exchange("sp", lambda _: mine, sp_full)
+        for piece in range(pieces):
+            half[piece * count : (piece + 1) * count] = sp_full[piece]
+        exchange("pair", lambda _: half, pair_full)
+    else:
+        exchange("pair", lambda _: mine, pair_full)
+    total[...] = pair_full[...]
+
+
+def summed(rows, scale, collective_id):
+    sp, grp = lax.axis_size("sp"), lax.axis_size("grp")
+    half, width = rows.shape[0] // 2, rows.shape[1]
+    scatter = half % (8 * sp) == 0
+    pieces = sp if scatter else 1
+    count = half // pieces
+    copies = 2 + 2 * (sp - 1) + (grp - 1)
+
+    def buffer(*shape):
+        return pltpu.VMEM(shape + (width,), jnp.float32)
+
+    total = pl.pallas_call(
+        functools.partial(sum_kernel, scatter, scale),
+        in_specs=[pl.BlockSpec(memory_space=pltpu.VMEM)],
+        out_specs=pl.BlockSpec(memory_space=pltpu.VMEM),
+        out_shape=jax.ShapeDtypeStruct((2, half, width), jnp.float32),
+        scratch_shapes=[
+            buffer(2, half),
+            buffer(pieces, count),
+            buffer(sp, count),
+            buffer(count),
+            buffer(grp, count),
+            buffer(count),
+            buffer(sp, count),
+            buffer(half),
+            buffer(2, half),
+            pltpu.SemaphoreType.DMA((copies,)),
+            pltpu.SemaphoreType.DMA((copies,)),
+        ],
+        compiler_params=pltpu.CompilerParams(
+            collective_id=collective_id, has_side_effects=True, vmem_limit_bytes=32 * 1024 * 1024
+        ),
+        name="sum_gradients_%d" % collective_id,
+    )(rows.reshape(2, half, width))
+    return total.reshape(rows.shape)
 
 
 def whole(shape):
@@ -519,8 +602,10 @@
         weight_qkv,
     )
     inv_count = 1.0 / math.sqrt(2 * windows * holders * window_len)
-    tail_sums = (lax.psum(tail_grads, ALL) * inv_count).reshape(2 + 2 * blocks, width, width)
-
+    early = jnp.concatenate([tail_grads, value_grads, jnp.zeros_like(value_grads)], axis=0)
+    tail_sums = summed(early, inv_count, 0).reshape(4 + 2 * blocks, width, width)
+
+    returned_keys, tail_sums = lax.optimization_barrier((returned_keys, tail_sums))
     grad_rows, key_grads = pl.pallas_call(
         key_kernel,
         grid_spec=pltpu.PrefetchScalarGridSpec(
@@ -545,15 +630,15 @@
         tokens[0],
         weight_qkv,
     )
-    kv_sums = summed(jnp.concatenate([key_grads, value_grads], axis=0)) * inv_count
+    key_sums = summed(key_grads, inv_count, 1)
 
     return (
         out_rows.reshape(1, windows, window_len, width),
         grad_rows[None],
-        jnp.concatenate([tail_sums[0], kv_sums[:width], kv_sums[width:]], axis=1),
+        jnp.concatenate([tail_sums[0], key_sums, tail_sums[2 + 2 * blocks]], axis=1),
         tail_sums[1],
         tail_sums[2 : 2 + blocks].transpose(1, 0, 2).reshape(width, hidden),
-        tail_sums[2 + blocks :].reshape(hidden, width),
+        tail_sums[2 + blocks : 2 + 2 * blocks].reshape(hidden, width),
     )
 
 

time: 517 us -> 455 us (0.88)
  waiting for transfers between devices: 190 us -> 63.4 us
  Pallas kernels: 136 us -> 238 us
  starting transfers between devices: 49 us -> 25.9 us
  between operations: 14.2 us -> 0.77 us
    pallas_call x0 -> x2, Pallas kernels: none -> 102 us  [summed(): pl.pallas_call(functools.partial(sum_kernel, scatter, scale), in_specs=[p...]
    all_to_all x2, waiting for transfers between devices: 103 us -> 41.2 us  [deliver(): lax.all_to_all(parcel, ('grp', 'sp'), split_axis=0, concat_axis=0, tiled=...]
    psum x1 -> x0, waiting for transfers between devices: 57.9 us -> none  [body(): lax.psum(tail_grads, ALL) * inv_count]
    all_to_all x2 -> x0, starting transfers between devices: 23 us -> none  [the longest x1 19.4 us: summed(): lax.all_to_all(rows.reshape(devices, rows.shape[0] // devices, rows.shape...]
    all_to_all x2 -> x0, waiting for transfers between devices: 5.81 us -> none  [the longest x1 5.8 us: summed(): lax.all_to_all(copies, ALL, split_axis=0, concat_axis=0, tiled=True)]
  transfers between devices with their start and end apart: 9 -> 6, of which waited for: 8 -> 5; matrix products, arithmetic and copies ran while one was open for 1% -> 0% of each run, Pallas kernels for 14% -> 31%
where the time goes in v3:
time: 455 us; the launch traced here: 454 us
  Pallas kernels  238 us (52%)
  blocking collectives  112 us (25%)
  waiting for transfers between devices  63.4 us (14%)
  starting transfers between devices  25.9 us (6%)
  local copies, waits for them, and re-layouts  9.2 us (2%)
    all_to_all x2, blocking collectives, deliver(): lax.all_to_all(parcel, ('grp', 'sp'), split_axis=0, concat_axis=0, tiled=...  112 us
    pallas_call x2, Pallas kernels, summed(): pl.pallas_call(functools.partial(sum_kernel, scatter, scale), in_specs=[p...  102 us
    pallas_call x1, Pallas kernels, body(): pl.pallas_call(first_kernel, grid_spec=pltpu.PrefetchScalarGridSpec(num_s...  57.2 us
    all_to_all x2, waiting for transfers between devices, deliver(): lax.all_to_all(parcel, ('grp', 'sp'), split_axis=0, concat_axis=0, tiled=...  41.2 us
    pallas_call x1, Pallas kernels, body(): pl.pallas_call(second_kernel, grid_spec=pltpu.PrefetchScalarGridSpec(num_...  32.1 us
    all_to_all x2, starting transfers between devices, deliver(): lax.all_to_all(parcel, ('grp', 'sp'), split_axis=0, concat_axis=0, tiled=...  25.1 us
    ppermute x4, waiting for transfers between devices, swapped(): return lax.ppermute(value, 'pair', [(0, 1), (1, 0)])  22.2 us
    pallas_call x1, Pallas kernels, body(): pl.pallas_call(key_kernel, grid_spec=pltpu.PrefetchScalarGridSpec(num_sca...  19.6 us
  transfers between devices with their start and end apart: 6, of which 5 were waited for; matrix products, arithmetic and copies ran while one was open for 0% of the time, Pallas kernels for 31%

profile of v3, /device:TPU:0, one launch (start us, length us, event | category | flops | bytes accessed | tf_op | source)
XLA Modules:
  0.0 453.7 jit_solution(13050626200731735235)
XLA Ops:
  0.6 0.8 copy.22
  1.4 0.7 broadcast_multiply_fusion
  2.9 0.8 copy.24
  3.8 1.0 scatter_custom_fusion
  4.9 0.5 collective-permute-start
  5.4 0.8 collective-permute-done
  6.2 15.3 %all_to_all.24 = s32[16,1,16]{2,1,0:T(1,128)S(1)} all-to-all(s32[16,1,16]{2,1,0:T(1,128)S(1)} %bitcast.56), channel_id=1, replica_groups=mesh['pair'=2,'grp'=4,'sp'=4] {'grp','sp'}, dimensions={0} | all-to-all | bytes 2048 | tf_op jit(solution)/shard_map/all_to_all | solution.py:323
  21.4 0.5 broadcast.38
  22.0 0.7 reduce.3
  22.6 0.6 reshape.99.wanted
  23.3 7.8 %pick.1 = bf16[256,64,128]{2,1,0:T(8,128)(2,1)} custom-call(s32[256]{0:T(256)} %reshape.99.wanted, bf16[64,64,128]{2,1,0:T(8,128)(2,1)} %bitcast.45), custom_call_target="tpu_custom_call" | custom-call | tf_op jit(solution)/shard_map/pick/pallas_call | solution.py:459
  31.1 96.9 %all_to_all.25 = bf16[16,16,64,128]{3,2,1,0:T(8,128)(2,1)S(1)} all-to-all(bf16[16,16,64,128]{3,2,1,0:T(8,128)(2,1)} %bitcast.44), channel_id=1, replica_groups=mesh['pair'=2,'grp'=4,'sp'=4] {'grp','sp'}, dimensions={0} | all-to-all | bytes 8388608 | tf_op jit(solution)/shard_map/all_to_all | solution.py:323
  128.0 0.5 multiply_add_fusion.position
  128.5 6.8 %collective-permute-done.1 = bf16[16,16,64,128]{3,2,1,0:T(8,128)(2,1)} collective-permute-done((bf16[16,16,64,128]{3,2,1,0:T(8,128)(2,1)S(1)}, bf16[16,16,64,128]{3,2,1,0:T(8,128)(2,1)}, u32[]{:S(2)}, u32[]{:S(2)}) %collective-permute-start.1) | collective-permute-done | bytes 4194336 | tf_op jit(solution)/shard_map/ppermute | solution.py:319
  135.3 57.2 %attend_and_tail.1 = (bf16[4096,128]{1,0:T(8,128)(2,1)}, bf16[4096,128]{1,0:T(8,128)(2,1)}, bf16[4096,512]{1,0:T(8,128)(2,1)}, bf16[4096,512]{1,0:T(8,128)(2,1)}...) custom-call(s32[128]{0:T(128)} %multiply_add_fusion.position, ...), custom_call_target="tpu_custom_call" | custom-call | tf_op jit(solution)/shard_map/attend_and_tail/pallas_call | solution.py:502
  192.7 7.2 %collective-permute-done.2 = bf16[16,16,64,128]{3,2,1,0:T(8,128)(2,1)S(1)} collective-permute-done((bf16[16,16,64,128]{3,2,1,0:T(8,128)(2,1)}, bf16[16,16,64,128]{3,2,1,0:T(8,128)(2,1)S(1)}, u32[]{:S(2)}, u32[]{:S(2)}) %collective-permute-start.2) | collective-permute-done | bytes 4194336 | tf_op jit(solution)/shard_map/ppermute | solution.py:319
  199.9 2.0 copy-done.1
  201.9 4.5 %all-to-all-start.2 = ((bf16[16,16,64,128]{3,2,1,0:T(8,128)(2,1)}), bf16[16,16,64,128]{3,2,1,0:T(8,128)(2,1)}, u32[]{:S(2)}, u32[]{:S(2)}) async-start(bf16[16,16,64,128]{3,2,1,0:T(8,128)(2,1)} %copy-done.1), calls=%async_computation.2 | async-start | bytes 8388608 | tf_op jit(solution)/shard_map/all_to_all | solution.py:323
  206.5 32.1 %key_gradients.1 = (bf16[4096,128]{1,0:T(8,128)(2,1)}, bf16[4096,128]{1,0:T(8,128)(2,1)}, f32[4096,128]{1,0:T(8,128)}, bf16[256,64,128]{2,1,0:T(8,128)(2,1)}, f32[1280,128]{1,0:T(8,128)}) custom-call(s32[128]{0:T(128)} %multiply_add_fusion.position, bf16[4096,128]{1,0:T(8,128)(2,1)} %bitcast.47, bf16[4096,128]{1,0:T(8,128)(2,1)} %bitcast.53, ...), custom_call_target="tpu_custom_call" | custom-call | flops 40000000000 | bytes 150000000 | tf_op jit(solution)/shard_map/key_gradients/pallas_call | solution.py:543
  238.8 7.4 %collective-permute-done.3 = bf16[16,16,64,128]{3,2,1,0:T(8,128)(2,1)} collective-permute-done((bf16[16,16,64,128]{3,2,1,0:T(8,128)(2,1)}, bf16[16,16,64,128]{3,2,1,0:T(8,128)(2,1)}, u32[]{:S(2)}, u32[]{:S(2)}) %collective-permute-start.3) | collective-permute-done | bytes 4194336 | tf_op jit(solution)/shard_map/ppermute | solution.py:319
  246.1 41.2 %all-to-all-done.2 = bf16[16,16,64,128]{3,2,1,0:T(8,128)(2,1)} async-done(((bf16[16,16,64,128]{3,2,1,0:T(8,128)(2,1)}), bf16[16,16,64,128]{3,2,1,0:T(8,128)(2,1)}, u32[]{:S(2)}, u32[]{:S(2)}) %all-to-all-start.2) | async-done | bytes 4194336 | tf_op jit(solution)/shard_map/all_to_all | solution.py:323
  287.3 20.6 %all-to-all-start.3 = ((bf16[16,16,64,128]{3,2,1,0:T(8,128)(2,1)}), bf16[16,16,64,128]{3,2,1,0:T(8,128)(2,1)}, u32[]{:S(2)}, u32[]{:S(2)}) async-start(bf16[16,16,64,128]{3,2,1,0:T(8,128)(2,1)} %collective-permute-done.3), calls=%async_computation.3 | async-start | bytes 8388608 | tf_op jit(solution)/shard_map/all_to_all | solution.py:323
  307.9 19.1 %collect_values.1 = (f32[64,64,128]{2,1,0:T(8,128)}, f32[128,128]{1,0:T(8,128)}) custom-call(s32[256]{0:T(256)} %reshape.99.wanted, bf16[256,64,128]{2,1,0:T(8,128)(2,1)} %bitcast.11.returned, f32[64,64,128]{2,1,0:T(8,128)} %bitcast.59, bf16[64,64,128]{2,1,0:T(8,128)(2,1)} %bitcast.62, bf16[64,64,128]{2,1,0:T(8,128)(2,1)} %bitcast.48, ...), custom_call_target="tpu_custom_call" | custom-call | flops 10000000000 | bytes 50000000 | tf_op jit(solution)/shard_map/collect_values/pallas_call | solution.py:578
  327.0 1.1 maximum_maximum_fusion
  328.1 87.4 %sum_gradients_0.1 = f32[2,768,128]{2,1,0:T(8,128)S(1)} custom-call(f32[2,768,128]{2,1,0:T(8,128)S(1)} %bitcast.39), custom_call_target="tpu_custom_call" | custom-call | tf_op jit(solution)/shard_map/sum_gradients_0/pallas_call | solution.py:400
  415.5 0.6 slice_bitcast_fusion.1
  416.1 0.7 fusion.4
  416.9 19.6 %collect_keys.1 = (bf16[64,64,128]{2,1,0:T(8,128)(2,1)}, f32[128,128]{1,0:T(8,128)}) custom-call(s32[256]{0:T(256)} %reshape.99.wanted, bf16[256,64,128]{2,1,0:T(8,128)(2,1)} %bitcast.12.returned, f32[64,64,128]{2,1,0:T(8,128)} %bitcast.51, f32[64,64,128]{2,1,0:T(8,128)} %get-tuple-element.76.upstream, f32[64,64,128]{2,1,0:T(8,128)} %bitcast.50, ...), custom_call_target="tpu_custom_call" | custom-call | tf_op jit(solution)/shard_map/collect_keys/pallas_call | solution.py:609
  436.5 0.8 copy-done
  437.3 14.9 %sum_gradients_1.1 = f32[2,64,128]{2,1,0:T(8,128)S(1)} custom-call(f32[2,64,128]{2,1,0:T(8,128)S(1)} %bitcast.43), custom_call_target="tpu_custom_call" | custom-call | tf_op jit(solution)/shard_map/sum_gradients_1/pallas_call | solution.py:400
  452.3 0.7 copy.28
  453.0 0.7 pad_maximum_fusion
  (19 shorter events, 1.4 us)
Async XLA Ops:
  4.9 1.3 collective-permute-start
  128.0 7.3 %collective-permute-start.1 = (bf16[16,16,64,128]{3,2,1,0:T(8,128)(2,1)S(1)}, bf16[16,16,64,128]{3,2,1,0:T(8,128)(2,1)}, u32[]{:S(2)}, u32[]{:S(2)}) collective-permute-start(bf16[16,16,64,128]{3,2,1,0:T(8,128)(2,1)S(1)} %all_to_all.25), channel_id=1, source_target_pairs={{0,16},{16,0},{1,17},{17,1},{2,18},{18,2},{3,19},{19,3},{4,20},{20... | collective-permute-start | bytes 12582920 | tf_op jit(solution)/shard_map/ppermute | solution.py:319
  192.5 7.4 %collective-permute-start.2 = (bf16[16,16,64,128]{3,2,1,0:T(8,128)(2,1)}, bf16[16,16,64,128]{3,2,1,0:T(8,128)(2,1)S(1)}, u32[]{:S(2)}, u32[]{:S(2)}) collective-permute-start(bf16[16,16,64,128]{3,2,1,0:T(8,128)(2,1)} %bitcast.58), channel_id=1, source_target_pairs={{0,16},{16,0},{1,17},{17,1},{2,18},{18,2},{3,19},{19,3},{4,20},{20... | collective-permute-start | bytes 12582920 | tf_op jit(solution)/shard_map/ppermute | solution.py:319
  199.9 2.0 copy-start.1
  201.9 85.4 %all-to-all-start.2 = ((bf16[16,16,64,128]{3,2,1,0:T(8,128)(2,1)}), bf16[16,16,64,128]{3,2,1,0:T(8,128)(2,1)}, u32[]{:S(2)}, u32[]{:S(2)}) async-start(bf16[16,16,64,128]{3,2,1,0:T(8,128)(2,1)} %copy-done.1), calls=%async_computation.2 | async-start | bytes 8388608 | tf_op jit(solution)/shard_map/all_to_all | solution.py:323
  238.6 7.6 %collective-permute-start.3 = (bf16[16,16,64,128]{3,2,1,0:T(8,128)(2,1)}, bf16[16,16,64,128]{3,2,1,0:T(8,128)(2,1)}, u32[]{:S(2)}, u32[]{:S(2)}) collective-permute-start(bf16[16,16,64,128]{3,2,1,0:T(8,128)(2,1)} %bitcast.57), channel_id=1, source_target_pairs={{0,16},{16,0},{1,17},{17,1},{2,18},{18,2},{3,19},{19,3},{4,20},{20... | collective-permute-start | bytes 12582920 | tf_op jit(solution)/shard_map/ppermute | solution.py:319
  287.3 128.2 %all-to-all-start.3 = ((bf16[16,16,64,128]{3,2,1,0:T(8,128)(2,1)}), bf16[16,16,64,128]{3,2,1,0:T(8,128)(2,1)}, u32[]{:S(2)}, u32[]{:S(2)}) async-start(bf16[16,16,64,128]{3,2,1,0:T(8,128)(2,1)} %collective-permute-done.3), calls=%async_computation.3 | async-start | bytes 8388608 | tf_op jit(solution)/shard_map/all_to_all | solution.py:323
  307.9 19.1 %copy-start.2 = (f32[1280,128]{1,0:T(8,128)S(1)}, f32[1280,128]{1,0:T(8,128)}, u32[]{:S(2)}) copy-start(f32[1280,128]{1,0:T(8,128)} %get-tuple-element.69) | copy-start | bytes 1966084
  436.5 0.8 copy-start

commit v4 on v3

--- a/solution.py
+++ b/solution.py
@@ -602,10 +602,6 @@
         weight_qkv,
     )
     inv_count = 1.0 / math.sqrt(2 * windows * holders * window_len)
-    early = jnp.concatenate([tail_grads, value_grads, jnp.zeros_like(value_grads)], axis=0)
-    tail_sums = summed(early, inv_count, 0).reshape(4 + 2 * blocks, width, width)
-
-    returned_keys, tail_sums = lax.optimization_barrier((returned_keys, tail_sums))
     grad_rows, key_grads = pl.pallas_call(
         key_kernel,
         grid_spec=pltpu.PrefetchScalarGridSpec(
@@ -630,12 +626,13 @@
         tokens[0],
         weight_qkv,
     )
-    key_sums = summed(key_grads, inv_count, 1)
+    all_grads = jnp.concatenate([tail_grads, value_grads, key_grads], axis=0)
+    tail_sums = summed(all_grads, inv_count, 0).reshape(4 + 2 * blocks, width, width)
 
     return (
         out_rows.reshape(1, windows, window_len, width),
         grad_rows[None],
-        jnp.concatenate([tail_sums[0], key_sums, tail_sums[2 + 2 * blocks]], axis=1),
+        jnp.concatenate([tail_sums[0], tail_sums[3 + 2 * blocks], tail_sums[2 + 2 * blocks]], axis=1),
         tail_sums[1],
         tail_sums[2 : 2 + blocks].transpose(1, 0, 2).reshape(width, hidden),
         tail_sums[2 + blocks : 2 + 2 * blocks].reshape(hidden, width),

time: 455 us -> 453 us (level)
  Pallas kernels: 238 us -> 177 us
  waiting for transfers between devices: 63.4 us -> 123 us
    pallas_call x2 -> x1, Pallas kernels: 102 us -> 41.6 us  [summed(): pl.pallas_call(functools.partial(sum_kernel, scatter, scale), in_specs=[p...]
    all_to_all x2, waiting for transfers between devices: 41.2 us -> 101 us  [deliver(): lax.all_to_all(parcel, ('grp', 'sp'), split_axis=0, concat_axis=0, tiled=...]
  transfers between devices with their start and end apart: 6 -> 6, of which waited for: 5 -> 6; matrix products, arithmetic and copies ran while one was open for 0% -> 0% of each run, Pallas kernels for 31% -> 11%
where the time goes in v4:
time: 453 us; the launch traced here: 452 us
  Pallas kernels  177 us (39%)
  waiting for transfers between devices  123 us (27%)
  blocking collectives  112 us (25%)
  starting transfers between devices  26 us (6%)
  local copies, waits for them, and re-layouts  8.36 us (2%)
    all_to_all x2, blocking collectives, deliver(): lax.all_to_all(parcel, ('grp', 'sp'), split_axis=0, concat_axis=0, tiled=...  112 us
    all_to_all x2, waiting for transfers between devices, deliver(): lax.all_to_all(parcel, ('grp', 'sp'), split_axis=0, concat_axis=0, tiled=...  101 us
    pallas_call x1, Pallas kernels, body(): pl.pallas_call(first_kernel, grid_spec=pltpu.PrefetchScalarGridSpec(num_s...  57.2 us
    pallas_call x1, Pallas kernels, summed(): pl.pallas_call(functools.partial(sum_kernel, scatter, scale), in_specs=[p...  41.6 us
    pallas_call x1, Pallas kernels, body(): pl.pallas_call(second_kernel, grid_spec=pltpu.PrefetchScalarGridSpec(num_...  32.1 us
    all_to_all x2, starting transfers between devices, deliver(): lax.all_to_all(parcel, ('grp', 'sp'), split_axis=0, concat_axis=0, tiled=...  25.1 us
    ppermute x4, waiting for transfers between devices, swapped(): return lax.ppermute(value, 'pair', [(0, 1), (1, 0)])  22.2 us
    pallas_call x1, Pallas kernels, body(): pl.pallas_call(key_kernel, grid_spec=pltpu.PrefetchScalarGridSpec(num_sca...  19.8 us
  transfers between devices with their start and end apart: 6, of which 6 were waited for; matrix products, arithmetic and copies ran while one was open for 0% of the time, Pallas kernels for 11%

profile of v4, /device:TPU:0, one launch (start us, length us, event | category | flops | bytes accessed | tf_op | source)
XLA Modules:
  0.0 451.7 jit_solution(1955680104658571547)
XLA Ops:
  0.6 0.7 broadcast_multiply_fusion
  1.3 0.8 copy.22
  2.3 0.8 copy.24
  3.8 1.0 scatter_custom_fusion
  4.9 0.5 collective-permute-start
  5.4 0.8 collective-permute-done
  6.2 15.3 %all_to_all.24 = s32[16,1,16]{2,1,0:T(1,128)S(1)} all-to-all(s32[16,1,16]{2,1,0:T(1,128)S(1)} %bitcast.55), channel_id=1, replica_groups=mesh['pair'=2,'grp'=4,'sp'=4] {'grp','sp'}, dimensions={0} | all-to-all | bytes 2048 | tf_op jit(solution)/shard_map/all_to_all | solution.py:323
  21.4 0.5 broadcast.36
  22.0 0.7 reduce.3
  22.6 0.6 reshape.93.wanted
  23.3 7.8 %pick.1 = bf16[256,64,128]{2,1,0:T(8,128)(2,1)} custom-call(s32[256]{0:T(256)} %reshape.93.wanted, bf16[64,64,128]{2,1,0:T(8,128)(2,1)} %bitcast.44), custom_call_target="tpu_custom_call" | custom-call | tf_op jit(solution)/shard_map/pick/pallas_call | solution.py:459
  31.1 96.9 %all_to_all.25 = bf16[16,16,64,128]{3,2,1,0:T(8,128)(2,1)S(1)} all-to-all(bf16[16,16,64,128]{3,2,1,0:T(8,128)(2,1)} %bitcast.43), channel_id=1, replica_groups=mesh['pair'=2,'grp'=4,'sp'=4] {'grp','sp'}, dimensions={0} | all-to-all | bytes 8388608 | tf_op jit(solution)/shard_map/all_to_all | solution.py:323
  128.0 0.5 multiply_add_fusion.position
  128.5 6.8 %collective-permute-done.1 = bf16[16,16,64,128]{3,2,1,0:T(8,128)(2,1)} collective-permute-done((bf16[16,16,64,128]{3,2,1,0:T(8,128)(2,1)S(1)}, bf16[16,16,64,128]{3,2,1,0:T(8,128)(2,1)}, u32[]{:S(2)}, u32[]{:S(2)}) %collective-permute-start.1) | collective-permute-done | bytes 4194336 | tf_op jit(solution)/shard_map/ppermute | solution.py:319
  135.3 57.2 %attend_and_tail.1 = (bf16[4096,128]{1,0:T(8,128)(2,1)}, bf16[4096,128]{1,0:T(8,128)(2,1)}, bf16[4096,512]{1,0:T(8,128)(2,1)}, bf16[4096,512]{1,0:T(8,128)(2,1)}...) custom-call(s32[128]{0:T(128)} %multiply_add_fusion.position, ...), custom_call_target="tpu_custom_call" | custom-call | tf_op jit(solution)/shard_map/attend_and_tail/pallas_call | solution.py:502
  192.5 0.2 collective-permute-start.2
  192.7 7.2 %collective-permute-done.2 = bf16[16,16,64,128]{3,2,1,0:T(8,128)(2,1)S(1)} collective-permute-done((bf16[16,16,64,128]{3,2,1,0:T(8,128)(2,1)}, bf16[16,16,64,128]{3,2,1,0:T(8,128)(2,1)S(1)}, u32[]{:S(2)}, u32[]{:S(2)}) %collective-permute-start.2) | collective-permute-done | bytes 4194336 | tf_op jit(solution)/shard_map/ppermute | solution.py:319
  199.9 2.0 copy-done
  201.9 4.5 %all-to-all-start.2 = ((bf16[16,16,64,128]{3,2,1,0:T(8,128)(2,1)}), bf16[16,16,64,128]{3,2,1,0:T(8,128)(2,1)}, u32[]{:S(2)}, u32[]{:S(2)}) async-start(bf16[16,16,64,128]{3,2,1,0:T(8,128)(2,1)} %copy-done), calls=%async_computation.2 | async-start | bytes 8388608 | tf_op jit(solution)/shard_map/all_to_all | solution.py:323
  206.4 32.1 %key_gradients.1 = (bf16[4096,128]{1,0:T(8,128)(2,1)}, bf16[4096,128]{1,0:T(8,128)(2,1)}, f32[4096,128]{1,0:T(8,128)}, bf16[256,64,128]{2,1,0:T(8,128)(2,1)}, f32[1280,128]{1,0:T(8,128)}) custom-call(s32[128]{0:T(128)} %multiply_add_fusion.position, bf16[4096,128]{1,0:T(8,128)(2,1)} %bitcast.46, bf16[4096,128]{1,0:T(8,128)(2,1)} %bitcast.52, ...), custom_call_target="tpu_custom_call" | custom-call | flops 40000000000 | bytes 150000000 | tf_op jit(solution)/shard_map/key_gradients/pallas_call | solution.py:543
  238.8 7.4 %collective-permute-done.3 = bf16[16,16,64,128]{3,2,1,0:T(8,128)(2,1)} collective-permute-done((bf16[16,16,64,128]{3,2,1,0:T(8,128)(2,1)}, bf16[16,16,64,128]{3,2,1,0:T(8,128)(2,1)}, u32[]{:S(2)}, u32[]{:S(2)}) %collective-permute-start.3) | collective-permute-done | bytes 4194336 | tf_op jit(solution)/shard_map/ppermute | solution.py:319
  246.1 41.2 %all-to-all-done.2 = bf16[16,16,64,128]{3,2,1,0:T(8,128)(2,1)} async-done(((bf16[16,16,64,128]{3,2,1,0:T(8,128)(2,1)}), bf16[16,16,64,128]{3,2,1,0:T(8,128)(2,1)}, u32[]{:S(2)}, u32[]{:S(2)}) %all-to-all-start.2) | async-done | bytes 4194336 | tf_op jit(solution)/shard_map/all_to_all | solution.py:323
  287.3 20.6 %all-to-all-start.3 = ((bf16[16,16,64,128]{3,2,1,0:T(8,128)(2,1)}), bf16[16,16,64,128]{3,2,1,0:T(8,128)(2,1)}, u32[]{:S(2)}, u32[]{:S(2)}) async-start(bf16[16,16,64,128]{3,2,1,0:T(8,128)(2,1)} %collective-permute-done.3), calls=%async_computation.3 | async-start | bytes 8388608 | tf_op jit(solution)/shard_map/all_to_all | solution.py:323
  307.8 19.0 %collect_values.1 = (f32[64,64,128]{2,1,0:T(8,128)}, f32[128,128]{1,0:T(8,128)}) custom-call(s32[256]{0:T(256)} %reshape.93.wanted, bf16[256,64,128]{2,1,0:T(8,128)(2,1)} %bitcast.11.returned, f32[64,64,128]{2,1,0:T(8,128)} %bitcast.58, bf16[64,64,128]{2,1,0:T(8,128)(2,1)} %bitcast.61, bf16[64,64,128]{2,1,0:T(8,128)(2,1)} %bitcast.47, ...), custom_call_target="tpu_custom_call" | custom-call | flops 10000000000 | bytes 50000000 | tf_op jit(solution)/shard_map/collect_values/pallas_call | solution.py:578
  326.9 59.7 %all-to-all-done.3 = bf16[16,16,64,128]{3,2,1,0:T(8,128)(2,1)} async-done(((bf16[16,16,64,128]{3,2,1,0:T(8,128)(2,1)}), bf16[16,16,64,128]{3,2,1,0:T(8,128)(2,1)}, u32[]{:S(2)}, u32[]{:S(2)}) %all-to-all-start.3) | async-done | bytes 4194336 | tf_op jit(solution)/shard_map/all_to_all | solution.py:323
  386.6 19.8 %collect_keys.1 = (bf16[64,64,128]{2,1,0:T(8,128)(2,1)}, f32[128,128]{1,0:T(8,128)}) custom-call(s32[256]{0:T(256)} %reshape.93.wanted, bf16[256,64,128]{2,1,0:T(8,128)(2,1)} %bitcast.12.returned, f32[64,64,128]{2,1,0:T(8,128)} %bitcast.50, f32[64,64,128]{2,1,0:T(8,128)} %get-tuple-element.71.upstream, f32[64,64,128]{2,1,0:T(8,128)} %bitcast.49, ...), custom_call_target="tpu_custom_call" | custom-call | tf_op jit(solution)/shard_map/collect_keys/pallas_call | solution.py:605
  406.3 0.9 pad_maximum_fusion
  407.2 41.6 %sum_gradients_0.1 = f32[2,768,128]{2,1,0:T(8,128)S(1)} custom-call(f32[2,768,128]{2,1,0:T(8,128)S(1)} %bitcast.42), custom_call_target="tpu_custom_call" | custom-call | tf_op jit(solution)/shard_map/sum_gradients_0/pallas_call | solution.py:400
  448.9 0.6 slice_bitcast_fusion.1
  449.5 0.7 fusion.4
  450.2 0.7 copy.28
  451.0 0.7 pad_maximum_fusion.1
  (16 shorter events, 1.2 us)
Async XLA Ops:
  4.9 1.3 collective-permute-start
  128.0 7.3 %collective-permute-start.1 = (bf16[16,16,64,128]{3,2,1,0:T(8,128)(2,1)S(1)}, bf16[16,16,64,128]{3,2,1,0:T(8,128)(2,1)}, u32[]{:S(2)}, u32[]{:S(2)}) collective-permute-start(bf16[16,16,64,128]{3,2,1,0:T(8,128)(2,1)S(1)} %all_to_all.25), channel_id=1, source_target_pairs={{0,16},{16,0},{1,17},{17,1},{2,18},{18,2},{3,19},{19,3},{4,20},{20... | collective-permute-start | bytes 12582920 | tf_op jit(solution)/shard_map/ppermute | solution.py:319
  192.5 7.4 %collective-permute-start.2 = (bf16[16,16,64,128]{3,2,1,0:T(8,128)(2,1)}, bf16[16,16,64,128]{3,2,1,0:T(8,128)(2,1)S(1)}, u32[]{:S(2)}, u32[]{:S(2)}) collective-permute-start(bf16[16,16,64,128]{3,2,1,0:T(8,128)(2,1)} %bitcast.57), channel_id=1, source_target_pairs={{0,16},{16,0},{1,17},{17,1},{2,18},{18,2},{3,19},{19,3},{4,20},{20... | collective-permute-start | bytes 12582920 | tf_op jit(solution)/shard_map/ppermute | solution.py:319
  199.9 2.0 copy-start
  201.9 85.4 %all-to-all-start.2 = ((bf16[16,16,64,128]{3,2,1,0:T(8,128)(2,1)}), bf16[16,16,64,128]{3,2,1,0:T(8,128)(2,1)}, u32[]{:S(2)}, u32[]{:S(2)}) async-start(bf16[16,16,64,128]{3,2,1,0:T(8,128)(2,1)} %copy-done), calls=%async_computation.2 | async-start | bytes 8388608 | tf_op jit(solution)/shard_map/all_to_all | solution.py:323
  238.5 7.6 %collective-permute-start.3 = (bf16[16,16,64,128]{3,2,1,0:T(8,128)(2,1)}, bf16[16,16,64,128]{3,2,1,0:T(8,128)(2,1)}, u32[]{:S(2)}, u32[]{:S(2)}) collective-permute-start(bf16[16,16,64,128]{3,2,1,0:T(8,128)(2,1)} %bitcast.56), channel_id=1, source_target_pairs={{0,16},{16,0},{1,17},{17,1},{2,18},{18,2},{3,19},{19,3},{4,20},{20... | collective-permute-start | bytes 12582920 | tf_op jit(solution)/shard_map/ppermute | solution.py:319
  287.3 99.3 %all-to-all-start.3 = ((bf16[16,16,64,128]{3,2,1,0:T(8,128)(2,1)}), bf16[16,16,64,128]{3,2,1,0:T(8,128)(2,1)}, u32[]{:S(2)}, u32[]{:S(2)}) async-start(bf16[16,16,64,128]{3,2,1,0:T(8,128)(2,1)} %collective-permute-done.3), calls=%async_computation.3 | async-start | bytes 8388608 | tf_op jit(solution)/shard_map/all_to_all | solution.py:323
  386.6 19.8 %copy-start.1 = (f32[1280,128]{1,0:T(8,128)S(1)}, f32[1280,128]{1,0:T(8,128)}, u32[]{:S(2)}) copy-start(f32[1280,128]{1,0:T(8,128)} %get-tuple-element.73) | copy-start | bytes 1966084
  386.6 19.8 %copy-start.2 = (f32[128,128]{1,0:T(8,128)S(1)}, f32[128,128]{1,0:T(8,128)}, u32[]{:S(2)}) copy-start(f32[128,128]{1,0:T(8,128)} %get-tuple-element.74) | copy-start | bytes 196612
